TPU v7x, 32 devices: a whole 2x2x4 slice. The times are simulated.
32 devices in a mesh: groups: 2 (over x), owner: 8 (over z, y), render: 2 (over core).
Axes of the slice: x: 2, y: 2, z: 4, core: 2. Of those that a mesh axis runs over, the one named last changes fastest.
Arguments:
- params: float32 [59, 131072], P(None, ('groups', 'owner', 'render')), parts along dimension 1
- first_moment: float32 [59, 131072], P(None, ('groups', 'owner', 'render')), parts along dimension 1, may hold values from -0.012 to 0.012
- second_moment: float32 [59, 131072], P(None, ('groups', 'owner', 'render')), parts along dimension 1, may hold values from 0.0001 to 0.1
- target: float32 [3, 512, 256], P(None, ('groups', 'owner', 'render')), parts along dimension 1, may hold values from 0 to 1
- view_yaw: float32 [32], P('groups'), parts along dimension 0, may hold values from -3.1416 to 3.1416, as said below
- tile_ids: int32 [512], P(('groups', 'owner', 'render')), parts along dimension 0, may hold values from 0 to 130559, as said below
- visible: int32 [32, 16, 256], P(('groups', 'owner', 'render')), parts along dimension 0, may hold values from 0 to 4095, as said below
- tile_slots: int32 [512, 256], P(('groups', 'owner', 'render')), parts along dimension 0, may hold values from 0 to 4095, as said below
- depth_rank: int32 [512, 256], P(('groups', 'owner', 'render')), parts along dimension 0, may hold values from 0 to 255, each once within a row
Outputs:
- new_params: float32 [59, 131072], P(None, ('groups', 'owner', 'render')), parts along dimension 1
- new_first: float32 [59, 131072], P(None, ('groups', 'owner', 'render')), parts along dimension 1
- new_second: float32 [59, 131072], P(None, ('groups', 'owner', 'render')), parts along dimension 1
- rendered: float32 [3, 512, 256], P(None, ('groups', 'owner', 'render')), parts along dimension 1
There are 2 independent parts, one for each index of `groups`. A program takes and returns all parts, laid end to end along the dimension named above; each array names one. Nothing has to cross between parts.
Inputs may be any that keep to these rules, and one draw needn't show every extreme that they name: `tile_ids`: distinct tiles of the 16 views; the 16 tiles of one device lie in one view. `view_yaw`: camera yaws, one a view. `visible`: for each device and owner, the first slots hold distinct local indices (used slots) and the rest hold 0 and are named by no list. No Gaussian is requested by two devices. Some owner gets all 256 slots used by every device, and every device uses all 256 slots for some owner. `tile_slots`: A slot o * 256 + s of the tile's device names its request visible[d, o, s]; every entry names a used slot, and every used slot of a device is named by one or two entries, in different tiles of that device. `depth_rank`: each row is a permutation.
All inputs are finite; a program needn't handle non-finite values.
Results may differ from a plain program's by a relative error of at most 0.0003.
Values sent between devices are 32-bit elements; how exact they have to be, the bound alone decides.
A program may use at most 64 MiB of HBM per device.

v0:
```python
import jax
import jax.numpy as jnp
from jax import lax
from jax.sharding import PartitionSpec as P

NPAR = 59
PIX = 256
ADAM_STEP = 10


tiles_view = 8160
tiles_across = 120
focal_len = 1000.0
distance = 4.0
beta_one = 0.9
beta_two = 0.999
adam_eps = 1e-15
harm_zero = 0.28209479177387814
harm_one = 0.4886025119029199
harm_two = (
    1.0925484305920792,
    -1.0925484305920792,
    0.31539156525252005,
    -1.0925484305920792,
    0.5462742152960396,
)
harm_three = (
    -0.5900435899266435,
    2.890611442640554,
    -0.4570457994644658,
    0.3731763325901154,
    -0.4570457994644658,
    1.445305721320277,
    -0.5900435899266435,
)


def harmonics(dir_x, dir_y, dir_z):
    sq_x = dir_x * dir_x
    sq_y = dir_y * dir_y
    sq_z = dir_z * dir_z
    terms = [
        jnp.full_like(dir_x, harm_zero),
        -harm_one * dir_y,
        harm_one * dir_z,
        -harm_one * dir_x,
        harm_two[0] * dir_x * dir_y,
        harm_two[1] * dir_y * dir_z,
        harm_two[2] * (2.0 * sq_z - sq_x - sq_y),
        harm_two[3] * dir_x * dir_z,
        harm_two[4] * (sq_x - sq_y),
        harm_three[0] * dir_y * (3.0 * sq_x - sq_y),
        harm_three[1] * dir_x * dir_y * dir_z,
        harm_three[2] * dir_y * (4.0 * sq_z - sq_x - sq_y),
        harm_three[3] * dir_z * (2.0 * sq_z - 3.0 * sq_x - 3.0 * sq_y),
        harm_three[4] * dir_x * (4.0 * sq_z - sq_x - sq_y),
        harm_three[5] * dir_z * (sq_x - sq_y),
        harm_three[6] * dir_x * (sq_x - 3.0 * sq_y),
    ]
    return jnp.stack(terms)


def quadratic(left_vec, covariance, right_vec):
    result = 0.0
    for first in range(3):
        for second in range(3):
            result = result + left_vec[first] * covariance[first][second] * right_vec[second]
    return result


def render_tiles(slot_rows, ordered, tile_ids, view_yaw):
    entries = slot_rows[:, ordered]
    view_index = tile_ids // tiles_view
    within = tile_ids % tiles_view
    anchor_x = (within % tiles_across * 16).astype(jnp.float32)
    anchor_y = (within // tiles_across * 16).astype(jnp.float32)
    onehot = (
        view_index[:, None] == jnp.arange(view_yaw.shape[0], dtype=jnp.int32)[None, :]
    ).astype(jnp.float32)
    yaw_tile = jnp.dot(onehot, view_yaw, precision=lax.Precision.HIGHEST)[:, None]
    cosine = jnp.cos(yaw_tile)
    sine_yaw = jnp.sin(yaw_tile)
    pos_x, pos_y, pos_z = (entries[0], entries[1], entries[2])
    cam_x = cosine * pos_x - sine_yaw * pos_z
    cam_z = sine_yaw * pos_x + cosine * pos_z + distance
    inverse_z = 1.0 / cam_z
    center_u = focal_len * cam_x * inverse_z + 960.0
    center_v = focal_len * pos_y * inverse_z + 540.0
    stretch = jnp.exp(entries[3:6])
    quaternion = entries[6:10]
    quaternion = quaternion / jnp.sqrt(jnp.sum(quaternion * quaternion, axis=0))
    quat_w, quat_x, quat_y, quat_z = (quaternion[0], quaternion[1], quaternion[2], quaternion[3])
    rotation = [
        [
            1.0 - 2.0 * (quat_y * quat_y + quat_z * quat_z),
            2.0 * (quat_x * quat_y - quat_w * quat_z),
            2.0 * (quat_x * quat_z + quat_w * quat_y),
        ],
        [
            2.0 * (quat_x * quat_y + quat_w * quat_z),
            1.0 - 2.0 * (quat_x * quat_x + quat_z * quat_z),
            2.0 * (quat_y * quat_z - quat_w * quat_x),
        ],
        [
            2.0 * (quat_x * quat_z - quat_w * quat_y),
            2.0 * (quat_y * quat_z + quat_w * quat_x),
            1.0 - 2.0 * (quat_x * quat_x + quat_y * quat_y),
        ],
    ]
    scaled = [[rotation[first][inner] * stretch[inner] for inner in range(3)] for first in range(3)]
    covariance = [
        [
            scaled[first][0] * scaled[second][0]
            + scaled[first][1] * scaled[second][1]
            + scaled[first][2] * scaled[second][2]
            for second in range(3)
        ]
        for first in range(3)
    ]
    focal_z = focal_len * inverse_z
    slope_x = focal_len * cam_x * inverse_z * inverse_z
    slope_y = focal_len * pos_y * inverse_z * inverse_z
    zeros_entry = jnp.zeros_like(focal_z)
    proj_u = [
        focal_z * cosine - slope_x * sine_yaw,
        zeros_entry,
        -focal_z * sine_yaw - slope_x * cosine,
    ]
    proj_v = [-slope_y * sine_yaw, focal_z, -slope_y * cosine]
    cov_a = quadratic(proj_u, covariance, proj_u) + 0.3
    cov_b = quadratic(proj_u, covariance, proj_v)
    cov_c = quadratic(proj_v, covariance, proj_v) + 0.3
    determinant = cov_a * cov_c - cov_b * cov_b
    conic_a = cov_c / determinant
    conic_b = -cov_b / determinant
    conic_c = cov_a / determinant
    opacity = jax.nn.sigmoid(entries[10])
    dir_x = pos_x + distance * sine_yaw
    dir_z = pos_z + distance * cosine
    length = jnp.sqrt(dir_x * dir_x + pos_y * pos_y + dir_z * dir_z)
    basis_set = harmonics(dir_x / length, pos_y / length, dir_z / length)
    coeffs = entries[11:].reshape(16, 3, entries.shape[1], entries.shape[2])
    colour = jax.nn.relu(jnp.sum(basis_set[:, None] * coeffs, axis=0) + 0.5)
    pixel_ids = jnp.arange(PIX, dtype=jnp.int32)
    pixel_x = anchor_x[:, None] + (pixel_ids % 16).astype(jnp.float32)[None, :] + 0.5
    pixel_y = anchor_y[:, None] + (pixel_ids // 16).astype(jnp.float32)[None, :] + 0.5
    delta_x = pixel_x[:, :, None] - center_u[:, None, :]
    delta_y = pixel_y[:, :, None] - center_v[:, None, :]
    exponent = -0.5 * (
        conic_a[:, None, :] * delta_x * delta_x
        + 2.0 * conic_b[:, None, :] * delta_x * delta_y
        + conic_c[:, None, :] * delta_y * delta_y
    )
    alphas = opacity[:, None, :] * jnp.exp(exponent)
    log_keep = jnp.log(1.0 - alphas)
    list_len = entries.shape[2]
    list_ids = jnp.arange(list_len, dtype=jnp.int32)
    upper_ones = (list_ids[:, None] < list_ids[None, :]).astype(jnp.float32)
    transmit = jnp.exp(
        jnp.einsum("tpj,jk->tpk", log_keep, upper_ones, precision=lax.Precision.HIGHEST)
    )
    weight = alphas * transmit
    return jnp.einsum("tpl,ctl->ctp", weight, colour, precision=lax.Precision.HIGHEST)


def step_rates():
    row_index = jnp.arange(NPAR, dtype=jnp.int32)[:, None]
    rates = jnp.where(
        row_index < 3,
        0.00016,
        jnp.where(
            row_index < 6,
            0.005,
            jnp.where(
                row_index < 10,
                0.001,
                jnp.where(row_index < 11, 0.05, jnp.where(row_index < 14, 0.0025, 0.000125)),
            ),
        ),
    )
    return rates.astype(jnp.float32)


def adam_update(params, moment, variance, gradient):
    moment = beta_one * moment + (1.0 - beta_one) * gradient
    variance = beta_two * variance + (1.0 - beta_two) * gradient * gradient
    fix_one = 1.0 - beta_one**ADAM_STEP
    fix_two = 1.0 - beta_two**ADAM_STEP
    params = params - step_rates() * (moment / fix_one) / (jnp.sqrt(variance / fix_two) + adam_eps)
    return (params, moment, variance)


def body(
    params, first_moment, second_moment, target, view_yaw, tile_ids, visible, tile_slots, depth_rank
):
    owners = lax.axis_size(("owner", "render"))
    slot_cap = visible.shape[2]
    requests = visible[0]
    wanted = lax.all_to_all(requests, ("owner", "render"), split_axis=0, concat_axis=0, tiled=True)
    row_list = wanted.reshape(-1)
    outgoing = jnp.take(params, row_list, axis=1).reshape(NPAR, owners, slot_cap)
    arrived = lax.all_to_all(outgoing, ("owner", "render"), split_axis=1, concat_axis=1, tiled=True)
    slot_rows = arrived.reshape(NPAR, owners * slot_cap)
    ordered = jnp.take_along_axis(tile_slots, depth_rank, axis=1)
    rendered, pullback = jax.vjp(
        lambda values: render_tiles(values, ordered, tile_ids, view_yaw), slot_rows
    )
    loss_scale = 1.0 / PIX
    (grad_rows,) = pullback((rendered - target) * loss_scale)
    outbound = grad_rows.reshape(NPAR, owners, slot_cap)
    returned = lax.all_to_all(
        outbound, ("owner", "render"), split_axis=1, concat_axis=1, tiled=True
    ).reshape(NPAR, owners * slot_cap)
    grad_total = jnp.zeros((NPAR, params.shape[1]), jnp.float32).at[:, row_list].add(returned)
    new_params, new_first, new_second = adam_update(params, first_moment, second_moment, grad_total)
    return (new_params, new_first, new_second, rendered)


def solution(mesh):
    in_specs = (
        P(None, ("groups", "owner", "render")),
        P(None, ("groups", "owner", "render")),
        P(None, ("groups", "owner", "render")),
        P(None, ("groups", "owner", "render"), None),
        P("groups"),
        P(("groups", "owner", "render")),
        P(("groups", "owner", "render"), None, None),
        P(("groups", "owner", "render"), None),
        P(("groups", "owner", "render"), None),
    )
    out_specs = (
        P(None, ("groups", "owner", "render")),
        P(None, ("groups", "owner", "render")),
        P(None, ("groups", "owner", "render")),
        P(None, ("groups", "owner", "render"), None),
    )
    return jax.shard_map(body, mesh=mesh, in_specs=in_specs, out_specs=out_specs, check_vma=False)
```

profile of v0, /device:TPU:0, one launch (start us, length us, event | category | flops | bytes accessed | tf_op | source)
XLA Modules:
  0.0 230.6 jit_solution(1467573583699128502)
XLA Ops:
  0.6 1.3 all_to_all.12
  2.0 7.4 %all-to-all-start = ((s32[16,1,256]{2,1,0:T(1,128)}), s32[16,1,256]{2,1,0:T(1,128)S(1)}, u32[]{:S(2)}, u32[]{:S(2)}) async-start(s32[16,1,256]{2,1,0:T(1,128)} %all_to_all.12), calls=%async_computation | async-start | bytes 32768 | tf_op jit(solution)/shard_map/all_to_all | solution.py:199
  10.1 32.8 %gather_fusion.2 = s32[4096]{0:T(1024)S(1)} fusion(s32[16,256]{1,0:T(8,128)S(1)} %copy-done, s32[4096]{0:T(1024)S(1)} %bitcast.305), kind=kCustom, calls=%fused_computation.2 | custom fusion | bytes 65536 | tf_op jit(solution)/shard_map/jit(take_along_axis)/gather | solution.py:204
  43.6 14.2 %gather_fusion = f32[4096,59]{1,0:T(8,128)} fusion(f32[59,4096]{0,1:T(8,128)S(1)} %copy.71, s32[4096]{0:T(1024)S(1)} %broadcast_clamp_fusion.1), kind=kCustom, calls=%fused_computation | custom fusion | bytes 1949696 | tf_op jit(solution)/shard_map/jit(_take)/gather | solution.py:201
  57.8 2.3 copy.72
  60.1 1.1 broadcast_select_fusion
  61.2 6.0 %all-to-all-start.1 = ((f32[59,16,256]{2,0,1:T(8,128)}), f32[59,16,256]{2,0,1:T(8,128)S(1)}, u32[]{:S(2)}, u32[]{:S(2)}) async-start(f32[59,16,256]{2,0,1:T(8,128)} %broadcast_select_fusion), calls=%async_computation.1 | async-start | bytes 2097152 | tf_op jit(solution)/shard_map/all_to_all | solution.py:202
  67.7 22.5 %all-to-all-done.1 = f32[59,16,256]{2,0,1:T(8,128)S(1)} async-done(((f32[59,16,256]{2,0,1:T(8,128)}), f32[59,16,256]{2,0,1:T(8,128)S(1)}, u32[]{:S(2)}, u32[]{:S(2)}) %all-to-all-start.1) | async-done | bytes 966688 | tf_op jit(solution)/shard_map/all_to_all | solution.py:202
  90.8 14.2 %gather_fusion.1 = f32[4096,59]{1,0:T(8,128)} fusion(f32[59,4096]{0,1:T(8,128)S(1)} %bitcast.306, s32[4096]{0:T(1024)S(1)} %broadcast_clamp_fusion), kind=kCustom, calls=%fused_computation.1 | custom fusion | bytes 1949696 | tf_op jit(solution)/shard_map/jvp()/gather | solution.py:72
  105.0 2.5 %copy.74 = f32[16,256,59]{1,0,2:T(8,128)S(1)} copy(f32[16,256,59]{2,1,0:T(8,128)} %bitcast.329) | data formatting | bytes 1933312 | tf_op jit(solution)/shard_map/jvp()/gather | solution.py:72
  108.6 4.4 %fusion.19 = f32[16,256,256]{2,1,0:T(8,128)S(1)} fusion(f32[16,256]{1,0:T(8,128)S(1)} %get-tuple-element.147, f32[16,256]{1,0:T(8,128)S(1)} %get-tuple-element.108, f32[16,256]{1,0:T(8,128)S(1)} %get-tuple-element.163, f32[16,256]{1,0:T(8,128)S(1)} %get-tuple-element.146, f32[16,256]{1,0:T(8,128)S(1)} %get-tuple-element.107, ...), kind=kOutput, calls=%fused_computation.38 | convolution fusion | flops 3234922496 | bytes 4325376 | tf_op jit(solution)/shard_map/jvp(tpj,jk->tpk)/dot_general | solution.py:160
  112.9 6.2 %fusion.34 = f32[3,16,256]{2,0,1:T(4,128)S(1)} fusion(f32[16,256,256]{2,1,0:T(8,128)S(1)} %fusion.19, f32[16,256]{1,0:T(8,128)S(1)} %get-tuple-element.147, f32[16,256]{1,0:T(8,128)S(1)} %get-tuple-element.108, f32[16,256]{1,0:T(8,128)S(1)} %get-tuple-element.163, f32[16,256]{1,0:T(8,128)S(1)} %get-tuple-element.146, f32[16,256]{1,0:T(8,128)S(1)} %get-tuple-element.107, ...), kind=kOutput, calls=%fused_computation.51 | convolution fusion | flops 51404800 | bytes 4423680 | tf_op jit(solution)/shard_map/jvp(tpl,ctl->ctp)/dot_general | solution.py:163
  119.2 5.3 %fusion.36 = f32[3,16,256]{2,0,1:T(4,128)S(1)} fusion(f32[16,256,256]{2,1,0:T(8,128)S(1)} %fusion.19, f32[16,256]{1,0:T(8,128)S(1)} %get-tuple-element.147, f32[16,256]{1,0:T(8,128)S(1)} %get-tuple-element.108, f32[16,256]{1,0:T(8,128)S(1)} %get-tuple-element.163, f32[16,256]{1,0:T(8,128)S(1)} %get-tuple-element.146, f32[16,256]{1,0:T(8,128)S(1)} %get-tuple-element.107, ...), kind=kOutput, calls=%fused_computation.53 | convolution fusion | flops 51441664 | bytes 4521984 | tf_op jit(solution)/shard_map/transpose(jvp(tpl,ctl->ctp))/dot_general | solution.py:163
  124.5 3.5 %fusion.45 = f32[16,256,256]{2,1,0:T(8,128)S(1)} fusion(f32[3,16,256]{2,1,0:T(8,128)S(1)} %multiply_reduce_fusion.2, f32[3,16,256]{2,0,1:T(4,128)S(1)} %fusion.34, f32[3,16,256]{2,1,0:T(8,128)S(1)} %copy-done.3), kind=kOutput, calls=%fused_computation.71 | convolution fusion | flops 37797888 | bytes 4341760 | tf_op jit(solution)/shard_map/transpose(jvp(tpl,ctl->ctp))/dot_general | solution.py:163
  128.1 11.5 %fusion.4 = (f32[16,256]{1,0:T(8,128)S(1)}, f32[16,256]{1,0:T(8,128)S(1)}, f32[16,256]{1,0:T(8,128)S(1)}, f32[16,256]{1,0:T(8,128)S(1)}, f32[16,256]{1,0:T(8,128)S(1)}, /*index=5*/f32[16,256]{1,0:T(8,128)S(1)}) fusion(f32[16,256]{1,0:T(8,128)S(1)} %get-tuple-element.147, f32[16,256]{1,0:T(8,128)S(1)} %get-tuple-element.108, ...), kind=kOutput, calls=%fused_computation.20 | convolution fusion | flops 3279986688 | bytes 8617984 | tf_op jit(solution)/shard_map/transpose(jvp(tpj,jk->tpk))/dot_general | solution.py:160
  140.7 2.1 copy.78
  142.7 23.2 %scatter_custom_fusion = f32[59,4096]{0,1:T(8,128)S(1)} fusion(s32[4096]{0:T(1024)S(1)} %bitcast.338, f32[4096,59]{1,0:T(8,128)} %bitcast.333, f32[]{:T(128)} %constant.58.clone.1), kind=kCustom, calls=%fused_computation.60 | custom fusion | flops 241664 | bytes 967168 | tf_op jit(solution)/shard_map/transpose(jvp())/scatter-add | solution.py:72
  165.9 1.6 copy.79
  167.5 6.9 %all-to-all-start.2 = ((f32[59,16,256]{2,0,1:T(8,128)}), f32[59,16,256]{2,0,1:T(8,128)S(1)}, u32[]{:S(2)}, u32[]{:S(2)}) async-start(f32[59,16,256]{2,0,1:T(8,128)} %copy.79), calls=%async_computation.2 | async-start | bytes 2097152 | tf_op jit(solution)/shard_map/all_to_all | solution.py:211
  175.0 22.3 %all-to-all-done.2 = f32[59,16,256]{2,0,1:T(8,128)S(1)} async-done(((f32[59,16,256]{2,0,1:T(8,128)}), f32[59,16,256]{2,0,1:T(8,128)S(1)}, u32[]{:S(2)}, u32[]{:S(2)}) %all-to-all-start.2) | async-done | bytes 966688 | tf_op jit(solution)/shard_map/all_to_all | solution.py:211
  198.6 2.0 copy.81
  200.6 24.5 %scatter_custom_fusion.1 = f32[59,4096]{0,1:T(8,128)S(1)} fusion(s32[4096]{0:T(1024)S(1)} %bitcast.336, f32[4096,59]{1,0:T(8,128)} %copy.81, f32[]{:T(128)} %constant.58.clone.1), kind=kCustom, calls=%fused_computation.58 | custom fusion | flops 241664 | bytes 967168 | tf_op jit(solution)/shard_map/scatter-add | solution.py:214
  225.1 1.6 copy.82
  226.7 3.9 %divide_subtract_fusion = (f32[59,4096]{1,0:T(8,128)}, f32[59,4096]{1,0:T(8,128)}, f32[59,4096]{1,0:T(8,128)}) fusion(f32[59,4096]{1,0:T(8,128)S(1)} %copy-done.2, f32[59]{0:T(128)S(1)} %fusion.168, f32[59,4096]{1,0:T(8,128)} %copy.82, f32[59,4096]{1,0:T(8,128)} %param.10, f32[59,4096]{1,0:T(8,128)} %param.11), kind=kLoop, calls=%fused_computation.56 | loop fusion | flops 2899968 | bytes 6766828 | tf_op jit(solution)/shard_map/sub | solution.py:189
  (83 shorter events, 6.4 us)
Async XLA Ops:
  0.6 9.5 %copy-start = (s32[16,256]{1,0:T(8,128)S(1)}, s32[16,256]{1,0:T(8,128)}, u32[]{:S(2)}) copy-start(s32[16,256]{1,0:T(8,128)} %param.16) | copy-start | bytes 49156
  2.0 41.6 %all-to-all-start = ((s32[16,1,256]{2,1,0:T(1,128)}), s32[16,1,256]{2,1,0:T(1,128)S(1)}, u32[]{:S(2)}, u32[]{:S(2)}) async-start(s32[16,1,256]{2,1,0:T(1,128)} %all_to_all.12), calls=%async_computation | async-start | bytes 32768 | tf_op jit(solution)/shard_map/all_to_all | solution.py:199
  10.1 32.8 %copy-start.1 = (f32[59,4096]{1,0:T(8,128)S(1)}, f32[59,4096]{1,0:T(8,128)}, u32[]{:S(2)}) copy-start(f32[59,4096]{1,0:T(8,128)} %param.9) | copy-start | bytes 2899972
  57.8 9.4 %copy-start.4 = (s32[16,256]{1,0:T(8,128)S(1)}, s32[16,256]{1,0:T(8,128)}, u32[]{:S(2)}) copy-start(s32[16,256]{1,0:T(8,128)} %param.17) | copy-start | bytes 49156
  57.8 9.5 %copy-start.5 = (s32[16]{0:T(128)S(1)}, s32[16]{0:T(128)}, u32[]{:S(2)}) copy-start(s32[16]{0:T(128)} %param.14) | copy-start | bytes 196
  57.8 9.5 %copy-start.6 = (f32[16]{0:T(128)S(1)}, f32[16]{0:T(128)}, u32[]{:S(2)}) copy-start(f32[16]{0:T(128)} %param.13) | copy-start | bytes 196
  61.2 29.0 %all-to-all-start.1 = ((f32[59,16,256]{2,0,1:T(8,128)}), f32[59,16,256]{2,0,1:T(8,128)S(1)}, u32[]{:S(2)}, u32[]{:S(2)}) async-start(f32[59,16,256]{2,0,1:T(8,128)} %broadcast_select_fusion), calls=%async_computation.1 | async-start | bytes 2097152 | tf_op jit(solution)/shard_map/all_to_all | solution.py:202
  112.9 6.3 %copy-start.3 = (f32[3,16,256]{2,1,0:T(8,128)S(1)}, f32[3,16,256]{2,1,0:T(8,128)}, u32[]{:S(2)}) copy-start(f32[3,16,256]{2,1,0:T(8,128)} %param.12) | copy-start | bytes 147460
  167.5 29.8 %all-to-all-start.2 = ((f32[59,16,256]{2,0,1:T(8,128)}), f32[59,16,256]{2,0,1:T(8,128)S(1)}, u32[]{:S(2)}, u32[]{:S(2)}) async-start(f32[59,16,256]{2,0,1:T(8,128)} %copy.79), calls=%async_computation.2 | async-start | bytes 2097152 | tf_op jit(solution)/shard_map/all_to_all | solution.py:211
  198.6 28.1 %copy-start.2 = (f32[59,4096]{1,0:T(8,128)S(1)}, f32[59,4096]{1,0:T(8,128)}, u32[]{:S(2)}) copy-start(f32[59,4096]{1,0:T(8,128)} %param.9) | copy-start | bytes 2899972
where the time goes:
time: 232 us; the launch traced here: 231 us
  local copies, waits for them, and re-layouts  77.7 us (33%)
  other arithmetic  55.5 us (24%)
  waiting for transfers between devices  44.8 us (19%)
  matrix products  31.1 us (13%)
  starting transfers between devices  20.3 us (9%)
    gather x2, local copies, waits for them, and re-layouts, body(): ordered = jnp.take_along_axis(tile_slots, depth_rank, axis=1)  32.8 us
    scatter-add x1, other arithmetic, body(): jnp.zeros((NPAR, params.shape[1]), jnp.float32).at[:, row_list]  24.5 us
    scatter-add x1, other arithmetic, render_tiles(): entries = slot_rows[:, ordered]  23.2 us
    all_to_all x1, waiting for transfers between devices, body(): lax.all_to_all(outgoing, ('owner', 'render'), split_axis=1, concat_axis=1...  22.5 us
    all_to_all x1, waiting for transfers between devices, body(): lax.all_to_all(outbound, ('owner', 'render'), split_axis=1, concat_axis=1...  22.3 us
    gather x2, local copies, waits for them, and re-layouts, render_tiles(): entries = slot_rows[:, ordered]  16.6 us
    gather x2, local copies, waits for them, and re-layouts, body(): jnp.take(params, row_list, axis=1).reshape(NPAR, owners, slot_cap)  16.4 us
    dot_general x2, matrix products, render_tiles(): jnp.einsum('tpj,jk->tpk', log_keep, upper_ones, precision=lax.Precision.H...  15.9 us
  transfers between devices with their start and end apart: 3, of which 2 were waited for; matrix products, arithmetic and copies ran while one was open for 15% of the time, Pallas kernels for 0%

commit v1 on v0

v1 whole, which is shorter than its diff:
```python
import functools

import jax
import jax.numpy as jnp
from jax import lax
from jax.experimental import pallas as pl
from jax.experimental.pallas import tpu as pltpu
from jax.sharding import PartitionSpec as P

NPAR = 59
PIX = 256
ADAM_STEP = 10
LANES = 128
QUANT = 9
SPLITS = 3

tiles_view = 8160
tiles_across = 120
focal_len = 1000.0
distance = 4.0
beta_one = 0.9
beta_two = 0.999
adam_eps = 1e-15
harm_zero = 0.28209479177387814
harm_one = 0.4886025119029199
harm_two = (
    1.0925484305920792,
    -1.0925484305920792,
    0.31539156525252005,
    -1.0925484305920792,
    0.5462742152960396,
)
harm_three = (
    -0.5900435899266435,
    2.890611442640554,
    -0.4570457994644658,
    0.3731763325901154,
    -0.4570457994644658,
    1.445305721320277,
    -0.5900435899266435,
)
VMEM = pltpu.CompilerParams(vmem_limit_bytes=56 * 1024 * 1024)
NN = (((1,), (0,)), ((), ()))
NT = (((1,), (1,)), ((), ()))


def mxu(left, right, dims=NN):
    return lax.dot_general(left, right, dims, preferred_element_type=jnp.float32)


def split_two(value):
    high = value.astype(jnp.bfloat16)
    low = (value - high.astype(jnp.float32)).astype(jnp.bfloat16)
    return high, low


def split_three(value):
    high = value.astype(jnp.bfloat16).astype(jnp.float32)
    rest = value - high
    mid = rest.astype(jnp.bfloat16).astype(jnp.float32)
    low = (rest - mid).astype(jnp.bfloat16).astype(jnp.float32)
    return high, mid, low


def harmonics(dir_x, dir_y, dir_z):
    sq_x = dir_x * dir_x
    sq_y = dir_y * dir_y
    sq_z = dir_z * dir_z
    return [
        jnp.full_like(dir_x, harm_zero),
        -harm_one * dir_y,
        harm_one * dir_z,
        -harm_one * dir_x,
        harm_two[0] * dir_x * dir_y,
        harm_two[1] * dir_y * dir_z,
        harm_two[2] * (2.0 * sq_z - sq_x - sq_y),
        harm_two[3] * dir_x * dir_z,
        harm_two[4] * (sq_x - sq_y),
        harm_three[0] * dir_y * (3.0 * sq_x - sq_y),
        harm_three[1] * dir_x * dir_y * dir_z,
        harm_three[2] * dir_y * (4.0 * sq_z - sq_x - sq_y),
        harm_three[3] * dir_z * (2.0 * sq_z - 3.0 * sq_x - 3.0 * sq_y),
        harm_three[4] * dir_x * (4.0 * sq_z - sq_x - sq_y),
        harm_three[5] * dir_z * (sq_x - sq_y),
        harm_three[6] * dir_x * (sq_x - 3.0 * sq_y),
    ]


def project(entries, cosine, sine_yaw):
    pos_x, pos_y, pos_z = entries[0], entries[1], entries[2]
    cam_x = cosine * pos_x - sine_yaw * pos_z
    cam_z = sine_yaw * pos_x + cosine * pos_z + distance
    inverse_z = 1.0 / cam_z
    center_u = focal_len * cam_x * inverse_z + 960.0
    center_v = focal_len * pos_y * inverse_z + 540.0
    stretch = [jnp.exp(entries[3 + axis]) for axis in range(3)]
    norm = entries[6] * entries[6] + entries[7] * entries[7]
    norm = norm + entries[8] * entries[8] + entries[9] * entries[9]
    inverse_norm = 1.0 / jnp.sqrt(norm)
    quat_w, quat_x, quat_y, quat_z = (entries[6 + part] * inverse_norm for part in range(4))
    rotation = [
        [
            1.0 - 2.0 * (quat_y * quat_y + quat_z * quat_z),
            2.0 * (quat_x * quat_y - quat_w * quat_z),
            2.0 * (quat_x * quat_z + quat_w * quat_y),
        ],
        [
            2.0 * (quat_x * quat_y + quat_w * quat_z),
            1.0 - 2.0 * (quat_x * quat_x + quat_z * quat_z),
            2.0 * (quat_y * quat_z - quat_w * quat_x),
        ],
        [
            2.0 * (quat_x * quat_z - quat_w * quat_y),
            2.0 * (quat_y * quat_z + quat_w * quat_x),
            1.0 - 2.0 * (quat_x * quat_x + quat_y * quat_y),
        ],
    ]
    focal_z = focal_len * inverse_z
    slope_x = focal_len * cam_x * inverse_z * inverse_z
    slope_y = focal_len * pos_y * inverse_z * inverse_z
    proj_u = [focal_z * cosine - slope_x * sine_yaw, None, -focal_z * sine_yaw - slope_x * cosine]
    proj_v = [-slope_y * sine_yaw, focal_z, -slope_y * cosine]
    left = [
        (proj_u[0] * rotation[0][axis] + proj_u[2] * rotation[2][axis]) * stretch[axis]
        for axis in range(3)
    ]
    right = [
        (
            proj_v[0] * rotation[0][axis]
            + proj_v[1] * rotation[1][axis]
            + proj_v[2] * rotation[2][axis]
        )
        * stretch[axis]
        for axis in range(3)
    ]
    cov_a = left[0] * left[0] + left[1] * left[1] + left[2] * left[2] + 0.3
    cov_b = left[0] * right[0] + left[1] * right[1] + left[2] * right[2]
    cov_c = right[0] * right[0] + right[1] * right[1] + right[2] * right[2] + 0.3
    determinant = cov_a * cov_c - cov_b * cov_b
    inverse_det = 1.0 / determinant
    conic_a = cov_c * inverse_det
    conic_b = -cov_b * inverse_det
    conic_c = cov_a * inverse_det
    logit = entries[10]
    tiny = logit < -80.0
    safe = jnp.where(tiny, 0.0, logit)
    log_opacity = jnp.where(tiny, logit, -jnp.log(1.0 + jnp.exp(-safe)))
    dir_x = pos_x + distance * sine_yaw
    dir_z = pos_z + distance * cosine
    inverse_len = 1.0 / jnp.sqrt(dir_x * dir_x + pos_y * pos_y + dir_z * dir_z)
    basis_set = harmonics(dir_x * inverse_len, pos_y * inverse_len, dir_z * inverse_len)
    colours = []
    for channel in range(3):
        total = basis_set[0] * entries[11 + channel]
        for term in range(1, 16):
            total = total + basis_set[term] * entries[11 + 3 * term + channel]
        total = total + 0.5
        colours.append(jnp.where(total > 0.0, total, 0.0))
    return [center_u, center_v, conic_a, conic_b, conic_c, log_opacity] + colours


def gather_columns(index, table_eight, table_one, chunks):
    low = index & (LANES - 1)
    high = lax.shift_right_logical(index, 7)
    eight = jnp.zeros((8, LANES), jnp.float32)
    one = jnp.zeros((8, LANES), jnp.float32)
    for chunk in range(chunks):
        here = high == chunk
        eight = jnp.where(here, lane_take(table_eight(chunk), low), eight)
        one = jnp.where(here, lane_take(table_one(chunk), low), one)
    return eight, one[0:1]


def lane_take(values, index):
    return jnp.take_along_axis(values, index, axis=1, mode="promise_in_bounds")


def scatter_columns(values, index, rows, total_ref):
    count = index.shape[1]
    low = index & (LANES - 1)
    high = lax.shift_right_logical(index, 7)
    low_hot = (lax.broadcasted_iota(jnp.int32, (LANES, count), 0) == low).astype(jnp.float32)
    low_hot = low_hot.astype(jnp.bfloat16)
    high_hot = lax.broadcasted_iota(jnp.int32, (rows, count), 0) == high
    for quantity in range(QUANT):
        pieces = [jnp.where(high_hot, part, 0.0) for part in split_three(values[quantity])]
        left = jnp.concatenate(pieces, axis=0).astype(jnp.bfloat16)
        sums = mxu(left, low_hot, NT)
        total_ref[pl.ds(quantity * rows, rows), :] += (
            sums[0:rows] + sums[rows : 2 * rows] + sums[2 * rows :]
        )


def load_entries(params_ref, scr, rows):
    chunks = params_ref.shape[1] // LANES
    for chunk in range(chunks):
        scr[pl.ds(chunk, NPAR, stride=rows), :] = params_ref[:, chunk * LANES : (chunk + 1) * LANES]
    scr[pl.ds(chunks, NPAR, stride=rows), :] = jnp.broadcast_to(params_ref[:, 0:1], (NPAR, LANES))
    return [scr[pl.ds(row * rows, rows), :] for row in range(NPAR)]


def owner_kernel(cap, rows, params_ref, column_ref, trig_ref, eight_ref, one_ref, yaw_ref, scr, table):
    slots = column_ref.shape[1]
    chunks = params_ref.shape[1] // LANES
    for row in range(NPAR):
        scr[pl.ds(row * rows, rows), :] = jnp.ones((rows, LANES), jnp.float32)
    column = column_ref[...]
    low_hot = lax.broadcasted_iota(jnp.int32, (LANES, slots), 0) == (column & (LANES - 1))
    high_hot = lax.broadcasted_iota(jnp.int32, (rows, slots), 0) == lax.shift_right_logical(column, 7)
    asker = (lax.broadcasted_iota(jnp.int32, (1, slots), 1) // cap).astype(jnp.float32)
    who = mxu(
        jnp.where(high_hot, asker, 0.0).astype(jnp.bfloat16),
        low_hot.astype(jnp.float32).astype(jnp.bfloat16),
        NT,
    ).astype(jnp.int32)
    row_ids = lax.broadcasted_iota(jnp.int32, (rows, LANES), 0)
    lane_ids = lax.broadcasted_iota(jnp.int32, (rows, LANES), 1)
    who = jnp.where(row_ids == chunks, lane_ids, who) & (LANES - 1)
    for part in range(2):
        known = jnp.broadcast_to(trig_ref[part : part + 1, :], (8, LANES))
        for block in range(rows // 8):
            yaw_ref[part, block * 8 : block * 8 + 8, :] = lane_take(
                known, who[block * 8 : block * 8 + 8]
            )
    entries = load_entries(params_ref, scr, rows)
    for quantity, value in enumerate(project(entries, yaw_ref[0], yaw_ref[1])):
        table[pl.ds(quantity * rows, rows), :] = value

    def table_eight(chunk):
        return table[pl.ds(chunk, 8, stride=rows), :]

    def table_one(chunk):
        return jnp.broadcast_to(table[pl.ds(8 * rows + chunk, 1), :], (8, LANES))

    @pl.loop(0, slots // LANES)
    def _(part):
        place = pl.ds(pl.multiple_of(part * LANES, LANES), LANES)
        index = jnp.broadcast_to(column_ref[:, place], (8, LANES))
        eight, one = gather_columns(index, table_eight, table_one, chunks + 1)
        eight_ref[:, place] = eight
        one_ref[:, place] = one


def tile_kernel(
    eight_ref,
    one_ref,
    slots_ref,
    rank_ref,
    anchor_ref,
    target_ref,
    out_ref,
    grad_eight_ref,
    grad_one_ref,
    total,
    weight_ref,
    ratio_ref,
    weight_high,
    weight_low,
    moment_high,
    moment_low,
):
    tiles, length = slots_ref.shape
    slots = eight_ref.shape[1]
    chunks = slots // LANES
    rows = chunks
    total[...] = jnp.zeros_like(total)
    def basis(shape, pixel_axis):
        pixel = lax.broadcasted_iota(jnp.int32, shape, pixel_axis)
        term = lax.broadcasted_iota(jnp.int32, shape, 1 - pixel_axis)
        px = (pixel & 15).astype(jnp.float32) - 7.5
        py = lax.shift_right_logical(pixel, 4).astype(jnp.float32) - 7.5
        kind = jnp.where(term < 24, term & 7, 7)
        value = jnp.where(kind == 0, 1.0, 0.0)
        value = jnp.where(kind == 1, px, value)
        value = jnp.where(kind == 2, py, value)
        value = jnp.where(kind == 3, px * px, value)
        value = jnp.where(kind == 4, px * py, value)
        value = jnp.where(kind == 5, py * py, value)
        return value.astype(jnp.bfloat16)

    basis_pixels = basis((PIX, 32), 0)
    basis_terms = basis((8, PIX), 1)
    from_ids = lax.broadcasted_iota(jnp.int32, (length, length), 0)
    to_ids = lax.broadcasted_iota(jnp.int32, (length, length), 1)
    before = (from_ids < to_ids).astype(jnp.float32).astype(jnp.bfloat16)
    after = (from_ids > to_ids).astype(jnp.float32).astype(jnp.bfloat16)

    def table_eight(chunk):
        return eight_ref[:, chunk * LANES : (chunk + 1) * LANES]

    def table_one(chunk):
        return jnp.broadcast_to(one_ref[:, chunk * LANES : (chunk + 1) * LANES], (8, LANES))

    step = 64

    @pl.loop(0, tiles)
    def _(tile):
        named = jnp.broadcast_to(slots_ref[pl.ds(tile, 1), :], (8, length))
        rank = jnp.broadcast_to(rank_ref[pl.ds(tile, 1), :], (8, length))
        halves = length // LANES
        ordered, eights, ones = [], [], []
        for half in range(halves):
            place = rank[:, half * LANES : (half + 1) * LANES]
            low = place & (LANES - 1)
            index = lane_take(named[:, 0:LANES], low)
            for other in range(1, halves):
                chosen = lane_take(named[:, other * LANES : (other + 1) * LANES], low)
                index = jnp.where(lax.shift_right_logical(place, 7) == other, chosen, index)
            eight, one = gather_columns(index, table_eight, table_one, chunks)
            ordered.append(index[0:1])
            eights.append(eight)
            ones.append(one)
        ordered = jnp.concatenate(ordered, axis=1)
        eight = jnp.concatenate(eights, axis=1)
        one = jnp.concatenate(ones, axis=1)
        off_u = eight[0:1] - anchor_ref[0, tile]
        off_v = eight[1:2] - anchor_ref[1, tile]
        con_a, con_b, con_c = eight[2:3], eight[3:4], eight[4:5]
        lin_x = con_a * off_u + con_b * off_v
        lin_y = con_b * off_u + con_c * off_v
        flat = eight[5:6] - 0.5 * (con_a * off_u * off_u + 2.0 * con_b * off_u * off_v + con_c * off_v * off_v)
        zero_row = jnp.zeros((1, length), jnp.float32)
        coefs = jnp.concatenate(
            [flat, lin_x, lin_y, -0.5 * con_a, -con_b, -0.5 * con_c, zero_row, zero_row], axis=0
        )
        zero_eight = jnp.zeros((8, length), jnp.float32)
        coefs = jnp.concatenate(list(split_three(coefs)) + [zero_eight], axis=0).astype(jnp.bfloat16)
        for part in range(PIX // step):
            span = slice(part * step, (part + 1) * step)
            alpha = jnp.exp(mxu(basis_pixels[span], coefs))
            keep = 1.0 - alpha
            high, low = split_two(jnp.log(keep))
            transmit = jnp.exp(mxu(high, before) + mxu(low, before))
            weight = alpha * transmit
            weight_ref[span, :] = weight
            ratio_ref[span, :] = alpha / keep
            high, low = split_two(weight)
            weight_high[span, :] = high
            weight_low[span, :] = low
        colour = jnp.concatenate([eight[6:8], one] + [zero_row] * 5, axis=0)
        col_h, col_m, col_l = split_three(colour)
        col_stack = jnp.concatenate([col_h, col_m, col_l, zero_eight], axis=0).astype(jnp.bfloat16)
        from_high = mxu(col_stack, weight_high[...], NT)
        from_low = mxu(col_stack, weight_low[...], NT)
        image = from_high[0:8] + (from_high[8:16] + from_low[0:8])
        image = image + (from_high[16:24] + from_low[8:16])
        wanted = []
        for channel in range(3):
            out_ref[channel, pl.ds(tile, 1), :] = image[channel : channel + 1]
            wanted.append(target_ref[channel, pl.ds(tile, 1), :])
        zero_pix = jnp.zeros((1, PIX), jnp.float32)
        wanted = jnp.concatenate(wanted + [zero_pix] * 5, axis=0)
        gradient = (image - wanted) * (1.0 / PIX)
        gr_h, gr_m, gr_l = split_three(gradient)
        zero_more = jnp.zeros((80, PIX), jnp.float32)
        gr_stack = jnp.concatenate([gr_h, gr_h, gr_h, gr_m, gr_m, gr_l, zero_more], axis=0)
        gr_turned = gr_stack.T.astype(jnp.bfloat16)
        zero_more = jnp.zeros((80, length), jnp.float32)
        col_all = jnp.concatenate([col_h, col_m, col_l, col_h, col_m, col_h, zero_more], axis=0)
        col_all = col_all.astype(jnp.bfloat16)
        for part in range(PIX // step):
            span = slice(part * step, (part + 1) * step)
            pull = mxu(gr_turned[span], col_all) * weight_ref[span, :]
            high, low = split_two(pull)
            behind = mxu(high, after) + mxu(low, after)
            high, low = split_two(pull - behind * ratio_ref[span, :])
            moment_high[span, :] = high
            moment_low[span, :] = low
        moments = mxu(basis_terms, moment_high[...]) + mxu(basis_terms, moment_low[...])
        gr_stack = jnp.concatenate([gr_h, gr_m, gr_l, jnp.zeros((8, PIX), jnp.float32)], axis=0)
        gr_stack = gr_stack.astype(jnp.bfloat16)
        from_high = mxu(gr_stack, weight_high[...])
        from_low = mxu(gr_stack, weight_low[...])
        d_colour = from_high[0:8] + (from_high[8:16] + from_low[0:8])
        d_colour = d_colour + (from_high[16:24] + from_low[8:16])
        m_0, m_x, m_y = moments[0:1], moments[1:2], moments[2:3]
        m_xx, m_xy, m_yy = moments[3:4], moments[4:5], moments[5:6]
        shift_x = m_x - off_u * m_0
        shift_y = m_y - off_v * m_0
        values = [
            con_a * shift_x + con_b * shift_y,
            con_b * shift_x + con_c * shift_y,
            -0.5 * (m_xx - off_u * (m_x + shift_x)),
            -(m_xy - off_u * m_y - off_v * shift_x),
            -0.5 * (m_yy - off_v * (m_y + shift_y)),
            m_0,
            d_colour[0:1],
            d_colour[1:2],
            d_colour[2:3],
        ]
        scatter_columns(values, ordered, rows, total)

    for chunk in range(chunks):
        grad_eight_ref[:, chunk * LANES : (chunk + 1) * LANES] = total[pl.ds(chunk, 8, stride=rows), :]
        grad_one_ref[:, chunk * LANES : (chunk + 1) * LANES] = total[pl.ds(8 * rows + chunk, 1), :]


def update_kernel(
    rows,
    params_ref,
    first_ref,
    second_ref,
    column_ref,
    yaw_ref,
    eight_ref,
    one_ref,
    new_params_ref,
    new_first_ref,
    new_second_ref,
    scr,
    total,
):
    slots = column_ref.shape[1]
    chunks = params_ref.shape[1] // LANES
    for row in range(NPAR):
        scr[pl.ds(row * rows, rows), :] = jnp.ones((rows, LANES), jnp.float32)
    total[...] = jnp.zeros_like(total)
    width = 256

    @pl.loop(0, slots // width)
    def _(part):
        place = pl.ds(pl.multiple_of(part * width, width), width)
        values = [eight_ref[pl.ds(row, 1), place] for row in range(8)] + [one_ref[:, place]]
        scatter_columns(values, column_ref[:, place], rows, total)

    entries = load_entries(params_ref, scr, rows)
    pulls = [total[pl.ds(quantity * rows, rows), :] for quantity in range(QUANT)]
    size = jnp.abs(pulls[0])
    for pull in pulls[1:]:
        size = jnp.maximum(size, jnp.abs(pull))
    touched = size > 0.0
    _, pullback = jax.vjp(lambda values: project(values, yaw_ref[0], yaw_ref[1]), entries)
    (gradients,) = pullback(pulls)
    for row in range(NPAR):
        scr[pl.ds(row * rows, rows), :] = jnp.where(touched, gradients[row], 0.0)
    extra = jnp.sum(scr[pl.ds(chunks, NPAR, stride=rows), :], axis=1, keepdims=True)
    lane = lax.broadcasted_iota(jnp.int32, (NPAR, LANES), 1)
    row_index = lax.broadcasted_iota(jnp.int32, (NPAR, LANES), 0)
    rates = jnp.where(row_index < 14, 0.0025, 0.000125)
    rates = jnp.where(row_index < 11, 0.05, rates)
    rates = jnp.where(row_index < 10, 0.001, rates)
    rates = jnp.where(row_index < 6, 0.005, rates)
    rates = jnp.where(row_index < 3, 0.00016, rates)
    fix_one = 1.0 - beta_one**ADAM_STEP
    fix_two = 1.0 - beta_two**ADAM_STEP
    for chunk in range(chunks):
        place = slice(chunk * LANES, (chunk + 1) * LANES)
        gradient = scr[pl.ds(chunk, NPAR, stride=rows), :]
        if chunk == 0:
            gradient = gradient + jnp.where(lane == 0, extra, 0.0)
        moment = beta_one * first_ref[:, place] + (1.0 - beta_one) * gradient
        variance = beta_two * second_ref[:, place] + (1.0 - beta_two) * gradient * gradient
        change = rates * (moment / fix_one) / (jnp.sqrt(variance / fix_two) + adam_eps)
        new_params_ref[:, place] = params_ref[:, place] - change
        new_first_ref[:, place] = moment
        new_second_ref[:, place] = variance


def exchange(values, owners, cap):
    rows = values.shape[0]
    sent = values.reshape(rows, owners, cap)
    got = lax.all_to_all(sent, ("owner", "render"), split_axis=1, concat_axis=1, tiled=True)
    return got.reshape(rows, owners * cap)


def body(
    params, first_moment, second_moment, target, view_yaw, tile_ids, visible, tile_slots, depth_rank
):
    owners = lax.axis_size(("owner", "render"))
    cap = visible.shape[2]
    slots = owners * cap
    held = params.shape[1]
    tiles, length = tile_slots.shape
    chunks = held // LANES
    rows = (chunks + 1 + 7) // 8 * 8
    f32 = jnp.float32
    view = tile_ids[0] // tiles_view
    requests = jnp.concatenate(
        [visible[0], jnp.full((owners, 1), view, jnp.int32)], axis=1
    )
    wanted = lax.all_to_all(requests, ("owner", "render"), split_axis=0, concat_axis=0, tiled=True)
    index = wanted[:, :cap]
    asker = jnp.arange(owners, dtype=jnp.int32)[:, None]
    column = jnp.where(index == 0, held + asker, index).reshape(1, slots)
    view_ids = jnp.arange(view_yaw.shape[0], dtype=jnp.int32)
    yaw = jnp.sum(jnp.where(wanted[:, cap][:, None] == view_ids[None, :], view_yaw[None, :], 0.0), axis=1)
    trig = jnp.stack([jnp.cos(yaw), jnp.sin(yaw)])
    trig = jnp.pad(trig, ((0, 6), (0, LANES - owners)))
    eight, one, yaws = pl.pallas_call(
        functools.partial(owner_kernel, cap, rows),
        out_shape=[
            jax.ShapeDtypeStruct((8, slots), f32),
            jax.ShapeDtypeStruct((1, slots), f32),
            jax.ShapeDtypeStruct((2, rows, LANES), f32),
        ],
        scratch_shapes=[pltpu.VMEM((NPAR * rows, LANES), f32), pltpu.VMEM((QUANT * rows, LANES), f32)],
        compiler_params=VMEM,
        name="owner_project",
    )(params, column, trig)
    both = exchange(jnp.concatenate([eight, one], axis=0), owners, cap)
    within = tile_ids % tiles_view
    anchors = jnp.stack([within % tiles_across, within // tiles_across]).astype(f32) * 16.0 + 8.0
    vmem = pl.BlockSpec(memory_space=pltpu.VMEM)
    rendered, grad_eight, grad_one = pl.pallas_call(
        tile_kernel,
        out_shape=[
            jax.ShapeDtypeStruct(target.shape, f32),
            jax.ShapeDtypeStruct((8, slots), f32),
            jax.ShapeDtypeStruct((1, slots), f32),
        ],
        in_specs=[vmem, vmem, vmem, vmem, pl.BlockSpec(memory_space=pltpu.SMEM), vmem],
        scratch_shapes=[
            pltpu.VMEM((QUANT * slots // LANES, LANES), f32),
            pltpu.VMEM((PIX, length), f32),
            pltpu.VMEM((PIX, length), f32),
            pltpu.VMEM((PIX, length), jnp.bfloat16),
            pltpu.VMEM((PIX, length), jnp.bfloat16),
            pltpu.VMEM((PIX, length), jnp.bfloat16),
            pltpu.VMEM((PIX, length), jnp.bfloat16),
        ],
        compiler_params=VMEM,
        name="tile_step",
    )(both[:8], both[8:], tile_slots, depth_rank, anchors, target)
    back = exchange(jnp.concatenate([grad_eight, grad_one], axis=0), owners, cap)
    new_params, new_first, new_second = pl.pallas_call(
        functools.partial(update_kernel, rows),
        out_shape=[jax.ShapeDtypeStruct(params.shape, f32)] * 3,
        scratch_shapes=[pltpu.VMEM((NPAR * rows, LANES), f32), pltpu.VMEM((QUANT * rows, LANES), f32)],
        compiler_params=VMEM,
        name="adam_step",
    )(params, first_moment, second_moment, column, yaws, back[:8], back[8:])
    return (new_params, new_first, new_second, rendered)


def solution(mesh):
    in_specs = (
        P(None, ("groups", "owner", "render")),
        P(None, ("groups", "owner", "render")),
        P(None, ("groups", "owner", "render")),
        P(None, ("groups", "owner", "render"), None),
        P("groups"),
        P(("groups", "owner", "render")),
        P(("groups", "owner", "render"), None, None),
        P(("groups", "owner", "render"), None),
        P(("groups", "owner", "render"), None),
    )
    out_specs = (
        P(None, ("groups", "owner", "render")),
        P(None, ("groups", "owner", "render")),
        P(None, ("groups", "owner", "render")),
        P(None, ("groups", "owner", "render"), None),
    )
    return jax.shard_map(body, mesh=mesh, in_specs=in_specs, out_specs=out_specs, check_vma=False)
```

time: 232 us -> 102 us (0.44)
  local copies, waits for them, and re-layouts: 77.7 us -> 5.71 us
  other arithmetic: 55.5 us -> 3.36 us
  Pallas kernels: 0 us -> 51.8 us
  matrix products: 31.1 us -> 0 us
  waiting for transfers between devices: 44.8 us -> 15.9 us
  blocking collectives: 0 us -> 12.8 us
  starting transfers between devices: 20.3 us -> 10.9 us
    gather x6 -> x0, local copies, waits for them, and re-layouts: 65.8 us -> none  [the longest x2 32.8 us: body(): ordered = jnp.take_along_axis(tile_slots, depth_rank, axis=1)]
    pallas_call x0 -> x3, Pallas kernels: none -> 51.8 us  [the longest x1 33.7 us: body(): pl.pallas_call(tile_kernel, out_shape=[jax.ShapeDtypeStruct(target.shape,...]
    scatter-add x2 -> x0, other arithmetic: 47.7 us -> none  [the longest x1 24.5 us: body(): jnp.zeros((NPAR, params.shape[1]), jnp.float32).at[:, row_list]]
    all_to_all x2 -> x1, waiting for transfers between devices: 44.7 us -> 9.4 us  [exchange(): lax.all_to_all(sent, ('owner', 'render'), split_axis=1, concat_axis=1, ti...]
    dot_general x6 -> x0, matrix products: 31.1 us -> none  [the longest x2 15.9 us: render_tiles(): jnp.einsum('tpj,jk->tpk', log_keep, upper_ones, precision=lax.Precision.H...]
    all_to_all x0 -> x1, blocking collectives: none -> 12.8 us  [exchange(): lax.all_to_all(sent, ('owner', 'render'), split_axis=1, concat_axis=1, ti...]
    all_to_all x2 -> x1, starting transfers between devices: 12.9 us -> 3.53 us  [exchange(): lax.all_to_all(sent, ('owner', 'render'), split_axis=1, concat_axis=1, ti...]
    all_to_all x1, waiting for transfers between devices: 0.01 us -> 6.53 us  [body(): lax.all_to_all(requests, ('owner', 'render'), split_axis=0, concat_axis=0...]
  transfers between devices with their start and end apart: 3 -> 2, of which waited for: 2 -> 2; matrix products, arithmetic and copies ran while one was open for 15% -> 1% of each run, Pallas kernels for 0% -> 0%
where the time goes in v1:
time: 102 us; the launch traced here: 101 us
  Pallas kernels  51.8 us (51%)
  waiting for transfers between devices  15.9 us (16%)
  blocking collectives  12.8 us (13%)
  starting transfers between devices  10.9 us (11%)
  local copies, waits for them, and re-layouts  5.71 us (6%)
  other arithmetic  3.36 us (3%)
    pallas_call x1, Pallas kernels, body(): pl.pallas_call(tile_kernel, out_shape=[jax.ShapeDtypeStruct(target.shape,...  33.7 us
    all_to_all x1, blocking collectives, exchange(): lax.all_to_all(sent, ('owner', 'render'), split_axis=1, concat_axis=1, ti...  12.8 us
    pallas_call x1, Pallas kernels, body(): pl.pallas_call(functools.partial(update_kernel, rows), out_shape=[jax.Sha...  10.8 us
    all_to_all x1, waiting for transfers between devices, exchange(): lax.all_to_all(sent, ('owner', 'render'), split_axis=1, concat_axis=1, ti...  9.4 us
    all_to_all x1, starting transfers between devices, body(): lax.all_to_all(requests, ('owner', 'render'), split_axis=0, concat_axis=0...  7.39 us
    pallas_call x1, Pallas kernels, body(): pl.pallas_call(functools.partial(owner_kernel, cap, rows), out_shape=[jax...  7.27 us
    all_to_all x1, waiting for transfers between devices, body(): lax.all_to_all(requests, ('owner', 'render'), split_axis=0, concat_axis=0...  6.53 us
    all_to_all x1, starting transfers between devices, exchange(): lax.all_to_all(sent, ('owner', 'render'), split_axis=1, concat_axis=1, ti...  3.53 us
  transfers between devices with their start and end apart: 2, of which 2 were waited for; matrix products, arithmetic and copies ran while one was open for 1% of the time, Pallas kernels for 0%

profile of v1, /device:TPU:0, one launch (start us, length us, event | category | flops | bytes accessed | tf_op | source)
XLA Modules:
  0.0 101.4 jit_solution(8428690539407863969)
XLA Ops:
  0.7 0.6 copy-done.1
  1.4 0.6 all_to_all.14
  2.1 7.4 %all-to-all-start = ((s32[16,1,257]{2,1,0:T(1,128)}), s32[16,1,257]{2,1,0:T(1,128)S(1)}, u32[]{:S(2)}, u32[]{:S(2)}) async-start(s32[16,1,257]{2,1,0:T(1,128)} %all_to_all.14), calls=%async_computation | async-start | bytes 49152 | tf_op jit(solution)/shard_map/all_to_all | solution.py:481
  9.5 6.5 %all-to-all-done = s32[16,1,257]{2,1,0:T(1,128)S(1)} async-done(((s32[16,1,257]{2,1,0:T(1,128)}), s32[16,1,257]{2,1,0:T(1,128)S(1)}, u32[]{:S(2)}, u32[]{:S(2)}) %all-to-all-start) | async-done | bytes 16480 | tf_op jit(solution)/shard_map/all_to_all | solution.py:481
  16.0 0.1 slice_reduce_fusion
  16.2 0.6 copy.18
  16.9 0.2 select_reduce_fusion
  17.1 0.6 select_maximum_fusion.trig_ref
  17.7 7.3 %owner_project.1 = (f32[8,4096]{1,0:T(8,128)}, f32[1,4096]{1,0:T(1,128)}, f32[2,40,128]{2,1,0:T(8,128)}) custom-call(f32[59,4096]{1,0:T(8,128)} %params_ref.3, s32[1,4096]{1,0:T(1,128)} %bitcast.35, f32[8,128]{1,0:T(8,128)} %select_maximum_fusion.trig_ref), custom_call_target="tpu_custom_call" | custom-call | tf_op jit(solution)/shard_map/owner_project/pallas_call | solution.py:489
  25.0 0.9 pad_maximum_fusion
  25.9 0.1 copy.19
  26.0 0.8 copy.15
  26.8 3.5 %all-to-all-start.1 = ((f32[9,16,256]{2,0,1:T(8,128)}), f32[9,16,256]{2,0,1:T(8,128)S(1)}, u32[]{:S(2)}, u32[]{:S(2)}) async-start(f32[9,16,256]{2,0,1:T(8,128)} %copy.15), calls=%async_computation.1 | async-start | bytes 524288 | tf_op jit(solution)/shard_map/all_to_all | solution.py:462
  30.4 0.6 fusion.2.anchor_ref
  31.0 9.4 %all-to-all-done.1 = f32[9,16,256]{2,0,1:T(8,128)S(1)} async-done(((f32[9,16,256]{2,0,1:T(8,128)}), f32[9,16,256]{2,0,1:T(8,128)S(1)}, u32[]{:S(2)}, u32[]{:S(2)}) %all-to-all-start.1) | async-done | bytes 147488 | tf_op jit(solution)/shard_map/all_to_all | solution.py:462
  40.4 0.6 slice.47
  41.0 0.7 slice.46
  41.7 33.7 %tile_step.1 = (f32[3,16,256]{2,1,0:T(8,128)}, f32[8,4096]{1,0:T(8,128)}, f32[1,4096]{1,0:T(1,128)}) custom-call(f32[8,4096]{1,0:T(8,128)} %bitcast.34, f32[1,4096]{1,0:T(1,128)} %bitcast.40, s32[16,256]{1,0:T(8,128)} %slots_ref.1, s32[16,256]{1,0:T(8,128)} %rank_ref.1, f32[2,16]{1,0:T(2,128)} %fusion.2.anchor_ref, f32[3,16,256]{2,1,0:T(8,128)} %target_ref.1), custom_call_target="tpu_custom_call" | custom-call | tf_op jit(solution)/shard_map/tile_step/pallas_call | solution.py:504
  75.4 0.9 pad_maximum_fusion.1
  76.5 0.1 copy.16
  76.6 12.8 %all_to_all.22 = f32[9,16,256]{2,0,1:T(8,128)S(1)} all-to-all(f32[9,16,256]{2,0,1:T(8,128)S(1)} %copy.16), channel_id=1, replica_groups=mesh['groups'=2,'owner'=8,'render'=2] {'owner','render'}, dimensions={1} | all-to-all | bytes 294912 | tf_op jit(solution)/shard_map/all_to_all | solution.py:462
  89.4 0.6 slice.49
  90.0 0.7 slice.48
  90.6 10.8 %adam_step.1 = (f32[59,4096]{1,0:T(8,128)}, f32[59,4096]{1,0:T(8,128)}, f32[59,4096]{1,0:T(8,128)}) custom-call(f32[59,4096]{1,0:T(8,128)} %params_ref.3, f32[59,4096]{1,0:T(8,128)} %first_ref.1, f32[59,4096]{1,0:T(8,128)} %second_ref.1, s32[1,4096]{1,0:T(1,128)} %bitcast.36, f32[2,40,128]{2,1,0:T(8,128)} %get-tuple-element.13.yaw_ref, f32[8,4096]{1,0:T(8,128)} %bitcast.33, ...), custom_call_target="tpu_custom_call" | custom-call | tf_op jit(solution)/shard_map/adam_step/pallas_call | solution.py:525
  (15 shorter events, 0.3 us)
Async XLA Ops:
  0.6 0.7 copy-start.1
  0.6 0.8 copy-start
  2.1 14.0 %all-to-all-start = ((s32[16,1,257]{2,1,0:T(1,128)}), s32[16,1,257]{2,1,0:T(1,128)S(1)}, u32[]{:S(2)}, u32[]{:S(2)}) async-start(s32[16,1,257]{2,1,0:T(1,128)} %all_to_all.14), calls=%async_computation | async-start | bytes 49152 | tf_op jit(solution)/shard_map/all_to_all | solution.py:481
  16.2 0.7 copy-start.2
  26.8 13.5 %all-to-all-start.1 = ((f32[9,16,256]{2,0,1:T(8,128)}), f32[9,16,256]{2,0,1:T(8,128)S(1)}, u32[]{:S(2)}, u32[]{:S(2)}) async-start(f32[9,16,256]{2,0,1:T(8,128)} %copy.15), calls=%async_computation.1 | async-start | bytes 524288 | tf_op jit(solution)/shard_map/all_to_all | solution.py:462

commit v2 on v1

--- a/solution.py
+++ b/solution.py
@@ -165,10 +165,11 @@
     eight = jnp.zeros((8, LANES), jnp.float32)
     one = jnp.zeros((8, LANES), jnp.float32)
     for chunk in range(chunks):
-        here = high == chunk
-        eight = jnp.where(here, lane_take(table_eight(chunk), low), eight)
-        one = jnp.where(here, lane_take(table_one(chunk), low), one)
-    return eight, one[0:1]
+        eight = jnp.where(high == chunk, lane_take(table_eight(chunk), low), eight)
+    inside = high - lax.broadcasted_iota(jnp.int32, (8, LANES), 0)
+    for block in range((chunks + 7) // 8):
+        one = jnp.where(inside == block * 8, lane_take(table_one(block), low), one)
+    return eight, jnp.sum(one, axis=0, keepdims=True)
 
 
 def lane_take(values, index):
@@ -182,13 +183,14 @@
     low_hot = (lax.broadcasted_iota(jnp.int32, (LANES, count), 0) == low).astype(jnp.float32)
     low_hot = low_hot.astype(jnp.bfloat16)
     high_hot = lax.broadcasted_iota(jnp.int32, (rows, count), 0) == high
-    for quantity in range(QUANT):
-        pieces = [jnp.where(high_hot, part, 0.0) for part in split_three(values[quantity])]
-        left = jnp.concatenate(pieces, axis=0).astype(jnp.bfloat16)
-        sums = mxu(left, low_hot, NT)
-        total_ref[pl.ds(quantity * rows, rows), :] += (
-            sums[0:rows] + sums[rows : 2 * rows] + sums[2 * rows :]
-        )
+    pieces = [split_two(value) for value in values]
+    left = [
+        jnp.where(high_hot, piece[part].astype(jnp.float32), 0.0)
+        for part in range(2)
+        for piece in pieces
+    ]
+    sums = mxu(jnp.concatenate(left, axis=0).astype(jnp.bfloat16), low_hot, NT)
+    total_ref[...] += sums[: QUANT * rows] + sums[QUANT * rows :]
 
 
 def load_entries(params_ref, scr, rows):
@@ -229,8 +231,8 @@
     def table_eight(chunk):
         return table[pl.ds(chunk, 8, stride=rows), :]
 
-    def table_one(chunk):
-        return jnp.broadcast_to(table[pl.ds(8 * rows + chunk, 1), :], (8, LANES))
+    def table_one(block):
+        return table[pl.ds(8 * rows + block * 8, 8), :]
 
     @pl.loop(0, slots // LANES)
     def _(part):
@@ -252,20 +254,19 @@
     grad_eight_ref,
     grad_one_ref,
     total,
-    weight_ref,
-    ratio_ref,
-    weight_high,
-    weight_low,
-    moment_high,
-    moment_low,
+    one_table,
+    *banks,
 ):
     tiles, length = slots_ref.shape
     slots = eight_ref.shape[1]
     chunks = slots // LANES
     rows = chunks
     total[...] = jnp.zeros_like(total)
+    for chunk in range(chunks):
+        one_table[chunk : chunk + 1, :] = one_ref[:, chunk * LANES : (chunk + 1) * LANES]
+
     def basis(shape, pixel_axis):
-        pixel = lax.broadcasted_iota(jnp.int32, shape, pixel_axis)
+        pixel = lax.broadcasted_iota(jnp.int32, shape, pixel_axis) & (PIX - 1)
         term = lax.broadcasted_iota(jnp.int32, shape, 1 - pixel_axis)
         px = (pixel & 15).astype(jnp.float32) - 7.5
         py = lax.shift_right_logical(pixel, 4).astype(jnp.float32) - 7.5
@@ -279,7 +280,7 @@
         return value.astype(jnp.bfloat16)
 
     basis_pixels = basis((PIX, 32), 0)
-    basis_terms = basis((8, PIX), 1)
+    basis_terms = basis((8, 2 * PIX), 1)
     from_ids = lax.broadcasted_iota(jnp.int32, (length, length), 0)
     to_ids = lax.broadcasted_iota(jnp.int32, (length, length), 1)
     before = (from_ids < to_ids).astype(jnp.float32).astype(jnp.bfloat16)
@@ -288,13 +289,10 @@
     def table_eight(chunk):
         return eight_ref[:, chunk * LANES : (chunk + 1) * LANES]
 
-    def table_one(chunk):
-        return jnp.broadcast_to(one_ref[:, chunk * LANES : (chunk + 1) * LANES], (8, LANES))
-
-    step = 64
-
-    @pl.loop(0, tiles)
-    def _(tile):
+    def table_one(block):
+        return one_table[block * 8 : block * 8 + 8, :]
+
+    def work(tile, weight_ref, ratio_ref, pair, weight_pair):
         named = jnp.broadcast_to(slots_ref[pl.ds(tile, 1), :], (8, length))
         rank = jnp.broadcast_to(rank_ref[pl.ds(tile, 1), :], (8, length))
         halves = length // LANES
@@ -325,25 +323,24 @@
         )
         zero_eight = jnp.zeros((8, length), jnp.float32)
         coefs = jnp.concatenate(list(split_three(coefs)) + [zero_eight], axis=0).astype(jnp.bfloat16)
-        for part in range(PIX // step):
-            span = slice(part * step, (part + 1) * step)
-            alpha = jnp.exp(mxu(basis_pixels[span], coefs))
-            keep = 1.0 - alpha
-            high, low = split_two(jnp.log(keep))
-            transmit = jnp.exp(mxu(high, before) + mxu(low, before))
-            weight = alpha * transmit
-            weight_ref[span, :] = weight
-            ratio_ref[span, :] = alpha / keep
-            high, low = split_two(weight)
-            weight_high[span, :] = high
-            weight_low[span, :] = low
+        yield
+        alpha = jnp.exp(mxu(basis_pixels, coefs))
+        weight_ref[...] = alpha
+        log_keep = jnp.log(1.0 - alpha)
+        ratio_ref[...] = alpha * jnp.exp(-log_keep)
+        pair[:PIX], pair[PIX:] = split_two(log_keep)
+        yield
+        logs = mxu(pair[...], before)
+        weight = weight_ref[...] * jnp.exp(logs[:PIX] + logs[PIX:])
+        weight_ref[...] = weight
+        weight_pair[:PIX], weight_pair[PIX:] = split_two(weight)
+        yield
         colour = jnp.concatenate([eight[6:8], one] + [zero_row] * 5, axis=0)
         col_h, col_m, col_l = split_three(colour)
         col_stack = jnp.concatenate([col_h, col_m, col_l, zero_eight], axis=0).astype(jnp.bfloat16)
-        from_high = mxu(col_stack, weight_high[...], NT)
-        from_low = mxu(col_stack, weight_low[...], NT)
-        image = from_high[0:8] + (from_high[8:16] + from_low[0:8])
-        image = image + (from_high[16:24] + from_low[8:16])
+        image = mxu(col_stack, weight_pair[...], NT)
+        image = image[:, :PIX] + image[:, PIX:]
+        image = image[0:8] + image[8:16] + image[16:24]
         wanted = []
         for channel in range(3):
             out_ref[channel, pl.ds(tile, 1), :] = image[channel : channel + 1]
@@ -358,21 +355,20 @@
         zero_more = jnp.zeros((80, length), jnp.float32)
         col_all = jnp.concatenate([col_h, col_m, col_l, col_h, col_m, col_h, zero_more], axis=0)
         col_all = col_all.astype(jnp.bfloat16)
-        for part in range(PIX // step):
-            span = slice(part * step, (part + 1) * step)
-            pull = mxu(gr_turned[span], col_all) * weight_ref[span, :]
-            high, low = split_two(pull)
-            behind = mxu(high, after) + mxu(low, after)
-            high, low = split_two(pull - behind * ratio_ref[span, :])
-            moment_high[span, :] = high
-            moment_low[span, :] = low
-        moments = mxu(basis_terms, moment_high[...]) + mxu(basis_terms, moment_low[...])
         gr_stack = jnp.concatenate([gr_h, gr_m, gr_l, jnp.zeros((8, PIX), jnp.float32)], axis=0)
-        gr_stack = gr_stack.astype(jnp.bfloat16)
-        from_high = mxu(gr_stack, weight_high[...])
-        from_low = mxu(gr_stack, weight_low[...])
-        d_colour = from_high[0:8] + (from_high[8:16] + from_low[0:8])
-        d_colour = d_colour + (from_high[16:24] + from_low[8:16])
+        gr_stack = jnp.concatenate([gr_stack, gr_stack], axis=1).astype(jnp.bfloat16)
+        yield
+        pull = mxu(gr_turned, col_all) * weight_ref[...]
+        weight_ref[...] = pull
+        pair[:PIX], pair[PIX:] = split_two(pull)
+        d_colour = mxu(gr_stack, weight_pair[...])
+        d_colour = d_colour[0:8] + d_colour[8:16] + d_colour[16:24]
+        yield
+        behind = mxu(pair[...], after)
+        pull = weight_ref[...] - (behind[:PIX] + behind[PIX:]) * ratio_ref[...]
+        weight_pair[:PIX], weight_pair[PIX:] = split_two(pull)
+        yield
+        moments = mxu(basis_terms, weight_pair[...])
         m_0, m_x, m_y = moments[0:1], moments[1:2], moments[2:3]
         m_xx, m_xy, m_yy = moments[3:4], moments[4:5], moments[5:6]
         shift_x = m_x - off_u * m_0
@@ -389,6 +385,18 @@
             d_colour[2:3],
         ]
         scatter_columns(values, ordered, rows, total)
+        yield
+
+    lanes = len(banks) // 4
+
+    @pl.loop(0, tiles // lanes)
+    def _(turn):
+        running = [
+            work(turn * lanes + lane, *banks[4 * lane : 4 * lane + 4]) for lane in range(lanes)
+        ]
+        for _ in range(7):
+            for one in running:
+                next(one)
 
     for chunk in range(chunks):
         grad_eight_ref[:, chunk * LANES : (chunk + 1) * LANES] = total[pl.ds(chunk, 8, stride=rows), :]
@@ -456,17 +464,72 @@
         new_second_ref[:, place] = variance
 
 
-def exchange(values, owners, cap):
-    rows = values.shape[0]
-    sent = values.reshape(rows, owners, cap)
+def exchange_kernel(owners, render, *refs):
+    count = (len(refs) - 2) // 2
+    sources, landings, (send_sem, recv_sem) = refs[:count], refs[count : 2 * count], refs[2 * count :]
+    me = lax.axis_index("owner") * render + lax.axis_index("render")
+
+    def place(ref, peer):
+        width = ref.shape[1] // owners
+        return ref.at[:, pl.ds(pl.multiple_of(peer * width, LANES), width)]
+
+    def where(step):
+        peer = lax.rem(me + step, owners)
+        return peer, {"owner": lax.div(peer, render), "render": lax.rem(peer, render)}
+
+    barrier = pltpu.get_barrier_semaphore()
+    for step in range(1, owners):
+        pl.semaphore_signal(
+            barrier, inc=1, device_id=where(step)[1], device_id_type=pl.DeviceIdType.MESH
+        )
+    pl.semaphore_wait(barrier, owners - 1)
+    copies = []
+    for step in range(1, owners):
+        peer, device = where(step)
+        for item in range(count):
+            copy = pltpu.make_async_remote_copy(
+                src_ref=place(sources[item], peer),
+                dst_ref=place(landings[item], me),
+                send_sem=send_sem.at[step, item],
+                recv_sem=recv_sem.at[step, item],
+                device_id=device,
+                device_id_type=pl.DeviceIdType.MESH,
+            )
+            copy.start()
+            copies.append(copy)
+    for item in range(count):
+        width = sources[item].shape[1] // owners
+        own = pl.ds(pl.multiple_of(me * width, LANES), width)
+        landings[item][:, own] = sources[item][:, own]
+    for copy in copies:
+        copy.wait()
+
+
+def exchange(arrays, owners, render, number):
+    if arrays[0].shape[1] // owners % LANES == 0:
+        vmem = pl.BlockSpec(memory_space=pltpu.VMEM)
+        return pl.pallas_call(
+            functools.partial(exchange_kernel, owners, render),
+            out_shape=[jax.ShapeDtypeStruct(each.shape, each.dtype) for each in arrays],
+            in_specs=[vmem] * len(arrays),
+            out_specs=[vmem] * len(arrays),
+            scratch_shapes=[pltpu.SemaphoreType.DMA((owners, len(arrays)))] * 2,
+            compiler_params=pltpu.CompilerParams(collective_id=number, has_side_effects=True),
+            name=f"exchange_{number}",
+        )(*arrays)
+    counts = [each.shape[0] for each in arrays]
+    values = jnp.concatenate(arrays, axis=0)
+    sent = values.reshape(values.shape[0], owners, -1)
     got = lax.all_to_all(sent, ("owner", "render"), split_axis=1, concat_axis=1, tiled=True)
-    return got.reshape(rows, owners * cap)
+    got = got.reshape(values.shape)
+    return [got[sum(counts[:item]) : sum(counts[: item + 1])] for item in range(len(arrays))]
 
 
 def body(
     params, first_moment, second_moment, target, view_yaw, tile_ids, visible, tile_slots, depth_rank
 ):
-    owners = lax.axis_size(("owner", "render"))
+    render = lax.axis_size("render")
+    owners = lax.axis_size("owner") * render
     cap = visible.shape[2]
     slots = owners * cap
     held = params.shape[1]
@@ -475,10 +538,10 @@
     rows = (chunks + 1 + 7) // 8 * 8
     f32 = jnp.float32
     view = tile_ids[0] // tiles_view
-    requests = jnp.concatenate(
-        [visible[0], jnp.full((owners, 1), view, jnp.int32)], axis=1
-    )
-    wanted = lax.all_to_all(requests, ("owner", "render"), split_axis=0, concat_axis=0, tiled=True)
+    spare = LANES if cap % LANES == 0 else 1
+    requests = jnp.concatenate([visible[0], jnp.full((owners, spare), view, jnp.int32)], axis=1)
+    (wanted,) = exchange([requests.reshape(1, -1)], owners, render, 0)
+    wanted = wanted.reshape(owners, cap + spare)
     index = wanted[:, :cap]
     asker = jnp.arange(owners, dtype=jnp.int32)[:, None]
     column = jnp.where(index == 0, held + asker, index).reshape(1, slots)
@@ -497,7 +560,7 @@
         compiler_params=VMEM,
         name="owner_project",
     )(params, column, trig)
-    both = exchange(jnp.concatenate([eight, one], axis=0), owners, cap)
+    eight, one = exchange([eight, one], owners, render, 1)
     within = tile_ids % tiles_view
     anchors = jnp.stack([within % tiles_across, within // tiles_across]).astype(f32) * 16.0 + 8.0
     vmem = pl.BlockSpec(memory_space=pltpu.VMEM)
@@ -511,24 +574,26 @@
         in_specs=[vmem, vmem, vmem, vmem, pl.BlockSpec(memory_space=pltpu.SMEM), vmem],
         scratch_shapes=[
             pltpu.VMEM((QUANT * slots // LANES, LANES), f32),
+            pltpu.VMEM((slots // LANES, LANES), f32),
+        ]
+        + [
             pltpu.VMEM((PIX, length), f32),
             pltpu.VMEM((PIX, length), f32),
-            pltpu.VMEM((PIX, length), jnp.bfloat16),
-            pltpu.VMEM((PIX, length), jnp.bfloat16),
-            pltpu.VMEM((PIX, length), jnp.bfloat16),
-            pltpu.VMEM((PIX, length), jnp.bfloat16),
-        ],
+            pltpu.VMEM((2 * PIX, length), jnp.bfloat16),
+            pltpu.VMEM((2 * PIX, length), jnp.bfloat16),
+        ]
+        * (2 if tiles % 2 == 0 else 1),
         compiler_params=VMEM,
         name="tile_step",
-    )(both[:8], both[8:], tile_slots, depth_rank, anchors, target)
-    back = exchange(jnp.concatenate([grad_eight, grad_one], axis=0), owners, cap)
+    )(eight, one, tile_slots, depth_rank, anchors, target)
+    grad_eight, grad_one = exchange([grad_eight, grad_one], owners, render, 2)
     new_params, new_first, new_second = pl.pallas_call(
         functools.partial(update_kernel, rows),
         out_shape=[jax.ShapeDtypeStruct(params.shape, f32)] * 3,
         scratch_shapes=[pltpu.VMEM((NPAR * rows, LANES), f32), pltpu.VMEM((QUANT * rows, LANES), f32)],
         compiler_params=VMEM,
         name="adam_step",
-    )(params, first_moment, second_moment, column, yaws, back[:8], back[8:])
+    )(params, first_moment, second_moment, column, yaws, grad_eight, grad_one)
     return (new_params, new_first, new_second, rendered)
 
 

time: 102 us -> 73.4 us (0.72)
  waiting for transfers between devices: 15.9 us -> 0 us
  Pallas kernels: 51.8 us -> 66 us
  blocking collectives: 12.8 us -> 0 us
  starting transfers between devices: 10.9 us -> 0 us
  local copies, waits for them, and re-layouts: 5.71 us -> 3.21 us
    pallas_call x0 -> x3, Pallas kernels: none -> 29.7 us  [exchange(): pl.pallas_call(functools.partial(exchange_kernel, owners, render), out_sh...]
    all_to_all x2 -> x0, waiting for transfers between devices: 15.9 us -> none  [the longest x1 9.4 us: exchange(): lax.all_to_all(sent, ('owner', 'render'), split_axis=1, concat_axis=1, ti...]
    pallas_call x1, Pallas kernels: 33.7 us -> 20.2 us  [body(): pl.pallas_call(tile_kernel, out_shape=[jax.ShapeDtypeStruct(target.shape,...]
    all_to_all x1 -> x0, blocking collectives: 12.8 us -> none  [exchange(): lax.all_to_all(sent, ('owner', 'render'), split_axis=1, concat_axis=1, ti...]
    all_to_all x2 -> x0, starting transfers between devices: 10.9 us -> none  [the longest x1 7.39 us: body(): lax.all_to_all(requests, ('owner', 'render'), split_axis=0, concat_axis=0...]
    slice x4 -> x0, local copies, waits for them, and re-layouts: 2.54 us -> none  [the longest x1 0.66 us: body(): both[:8]]
    concatenate x2 -> x0, other arithmetic: 1.88 us -> none  [the longest x1 0.94 us: body(): both = exchange(jnp.concatenate([eight, one], axis=0), owners, cap)]
    pallas_call x0 -> x1, other arithmetic: none -> 1.44 us  [exchange(): pl.pallas_call(functools.partial(exchange_kernel, owners, render), out_sh...]
  transfers between devices with their start and end apart: 2 -> 0, of which waited for: 2 -> 0; matrix products, arithmetic and copies ran while one was open for 1% -> 0% of each run, Pallas kernels for 0% -> 0%
where the time goes in v2:
time: 73.4 us; the launch traced here: 73 us
  Pallas kernels  66 us (90%)
  local copies, waits for them, and re-layouts  3.21 us (4%)
  other arithmetic  2.91 us (4%)
  between operations  0.83 us (1%)
    pallas_call x3, Pallas kernels, exchange(): pl.pallas_call(functools.partial(exchange_kernel, owners, render), out_sh...  29.7 us
    pallas_call x1, Pallas kernels, body(): pl.pallas_call(tile_kernel, out_shape=[jax.ShapeDtypeStruct(target.shape,...  20.2 us
    pallas_call x1, Pallas kernels, body(): pl.pallas_call(functools.partial(update_kernel, rows), out_shape=[jax.Sha...  9.7 us
    pallas_call x1, Pallas kernels, body(): pl.pallas_call(functools.partial(owner_kernel, cap, rows), out_shape=[jax...  6.35 us
    unnamed x10, local copies, waits for them, and re-layouts  2.64 us

profile of v2, /device:TPU:0, one launch (start us, length us, event | category | flops | bytes accessed | tf_op | source)
XLA Modules:
  0.0 73.0 jit_solution(10968989232973039748)
XLA Ops:
  0.6 0.0 copy-start.1
  0.6 0.6 copy-done.1
  1.3 0.0 copy-start
  1.5 0.6 fusion.2.anchor_ref
  2.0 0.0 copy-done
  2.0 0.6 copy.16
  2.7 9.9 %exchange_0.1 = s32[1,6144]{1,0:T(1,128)} custom-call(s32[1,6144]{1,0:T(1,128)} %bitcast.23), custom_call_target="tpu_custom_call" | custom-call | tf_op jit(solution)/shard_map/exchange_0/pallas_call | solution.py:511
  12.6 0.5 broadcast.37
  13.1 1.4 %reduce.3 = s32[6144]{0:T(1024)S(1)} reduce(s32[1,6144]{1,0:T(1,128)} %exchange_0.1, s32[]{:T(128)} %broadcast.37), dimensions={0}, to_apply=%pallas_call.44.reduce_sub_computation.3 | reduce | bytes 49156 | tf_op jit(solution)/shard_map/exchange_0/pallas_call | solution.py:511
  14.6 0.1 fusion
  14.7 0.1 copy.15
  14.7 0.0 copy-start.2
  14.7 0.7 copy-done.2
  15.4 0.2 select_reduce_fusion
  15.6 0.6 copy.17
  16.2 0.6 select_maximum_fusion.trig_ref
  16.8 6.4 %owner_project.1 = (f32[8,4096]{1,0:T(8,128)}, f32[1,4096]{1,0:T(1,128)}, f32[2,40,128]{2,1,0:T(8,128)}) custom-call(f32[59,4096]{1,0:T(8,128)} %params_ref.3, s32[1,4096]{1,0:T(1,128)} %bitcast.21, f32[8,128]{1,0:T(8,128)} %select_maximum_fusion.trig_ref), custom_call_target="tpu_custom_call" | custom-call | tf_op jit(solution)/shard_map/owner_project/pallas_call | solution.py:552
  23.2 9.6 %exchange_1.1 = (f32[8,4096]{1,0:T(8,128)}, f32[1,4096]{1,0:T(1,128)}) custom-call(f32[8,4096]{1,0:T(8,128)} %get-tuple-element.18.refs_0_, f32[1,4096]{1,0:T(1,128)} %get-tuple-element.19.refs_1_), custom_call_target="tpu_custom_call" | custom-call | tf_op jit(solution)/shard_map/exchange_1/pallas_call | solution.py:511
  32.8 20.2 %tile_step.1 = (f32[3,16,256]{2,1,0:T(8,128)}, f32[8,4096]{1,0:T(8,128)}, f32[1,4096]{1,0:T(1,128)}) custom-call(f32[8,4096]{1,0:T(8,128)} %get-tuple-element.20.eight_ref, f32[1,4096]{1,0:T(1,128)} %get-tuple-element.21.one_ref, s32[16,256]{1,0:T(8,128)} %slots_ref.1, s32[16,256]{1,0:T(8,128)} %rank_ref.1, f32[2,16]{1,0:T(2,128)} %fusion.2.anchor_ref, ...), custom_call_target="tpu_custom_call" | custom-call | tf_op jit(solution)/shard_map/tile_step/pallas_call | solution.py:567
  53.1 10.2 %exchange_2.1 = (f32[8,4096]{1,0:T(8,128)}, f32[1,4096]{1,0:T(1,128)}) custom-call(f32[8,4096]{1,0:T(8,128)} %get-tuple-element.22.refs_0_, f32[1,4096]{1,0:T(1,128)} %get-tuple-element.23.refs_1_), custom_call_target="tpu_custom_call" | custom-call | tf_op jit(solution)/shard_map/exchange_2/pallas_call | solution.py:511
  63.3 9.7 %adam_step.1 = (f32[59,4096]{1,0:T(8,128)}, f32[59,4096]{1,0:T(8,128)}, f32[59,4096]{1,0:T(8,128)}) custom-call(f32[59,4096]{1,0:T(8,128)} %params_ref.3, f32[59,4096]{1,0:T(8,128)} %first_ref.1, f32[59,4096]{1,0:T(8,128)} %second_ref.1, s32[1,4096]{1,0:T(1,128)} %bitcast.22, f32[2,40,128]{2,1,0:T(8,128)} %get-tuple-element.17.yaw_ref, ...), custom_call_target="tpu_custom_call" | custom-call | tf_op jit(solution)/shard_map/adam_step/pallas_call | solution.py:590
  (7 shorter events, 0.1 us)
Async XLA Ops:
  0.6 0.7 copy-start.1
  1.3 0.8 %copy-start = (s32[1,16,256]{2,1,0:T(8,128)S(1)}, s32[1,16,256]{2,1,0:T(8,128)}, u32[]{:S(2)}) copy-start(s32[1,16,256]{2,1,0:T(8,128)} %param.15) | copy-start | bytes 49156
  14.7 0.7 copy-start.2

commit v3 on v2

--- a/solution.py
+++ b/solution.py
@@ -193,6 +193,11 @@
     total_ref[...] += sums[: QUANT * rows] + sums[QUANT * rows :]
 
 
+def clear_entries(scr, rows):
+    for row in range(NPAR):
+        scr[pl.ds(row * rows + rows - 8, 8), :] = jnp.ones((8, LANES), jnp.float32)
+
+
 def load_entries(params_ref, scr, rows):
     chunks = params_ref.shape[1] // LANES
     for chunk in range(chunks):
@@ -201,11 +206,49 @@
     return [scr[pl.ds(row * rows, rows), :] for row in range(NPAR)]
 
 
-def owner_kernel(cap, rows, params_ref, column_ref, trig_ref, eight_ref, one_ref, yaw_ref, scr, table):
+class Peers:
+    def __init__(self, owners, render):
+        self.owners, self.render = owners, render
+        self.me = lax.axis_index("owner") * render + lax.axis_index("render")
+
+    def peer(self, step):
+        return lax.rem(self.me + step, self.owners)
+
+    def device(self, step):
+        peer = self.peer(step)
+        return {"owner": lax.div(peer, self.render), "render": lax.rem(peer, self.render)}
+
+    def greet(self):
+        barrier = pltpu.get_barrier_semaphore()
+        for step in range(1, self.owners):
+            pl.semaphore_signal(
+                barrier, inc=1, device_id=self.device(step), device_id_type=pl.DeviceIdType.MESH
+            )
+
+    def met(self):
+        pl.semaphore_wait(pltpu.get_barrier_semaphore(), self.owners - 1)
+
+    def place(self, ref, peer):
+        width = ref.shape[1] // self.owners
+        return ref.at[:, pl.ds(pl.multiple_of(peer * width, LANES), width)]
+
+    def copy(self, source, landing, sems, step, item):
+        return pltpu.make_async_remote_copy(
+            src_ref=self.place(source, self.peer(step)),
+            dst_ref=self.place(landing, self.me),
+            send_sem=sems[0].at[step, item],
+            recv_sem=sems[1].at[step, item],
+            device_id=self.device(step),
+            device_id_type=pl.DeviceIdType.MESH,
+        )
+
+    def keep(self, source, landing):
+        self.place(landing, self.me)[...] = self.place(source, self.me)[...]
+
+
+def project_all(cap, rows, params_ref, column_ref, views, trig, yaw_ref, scr, table):
     slots = column_ref.shape[1]
     chunks = params_ref.shape[1] // LANES
-    for row in range(NPAR):
-        scr[pl.ds(row * rows, rows), :] = jnp.ones((rows, LANES), jnp.float32)
     column = column_ref[...]
     low_hot = lax.broadcasted_iota(jnp.int32, (LANES, slots), 0) == (column & (LANES - 1))
     high_hot = lax.broadcasted_iota(jnp.int32, (rows, slots), 0) == lax.shift_right_logical(column, 7)
@@ -218,32 +261,117 @@
     row_ids = lax.broadcasted_iota(jnp.int32, (rows, LANES), 0)
     lane_ids = lax.broadcasted_iota(jnp.int32, (rows, LANES), 1)
     who = jnp.where(row_ids == chunks, lane_ids, who) & (LANES - 1)
+    known = lane_take(trig, jnp.broadcast_to(views, (8, LANES)))
     for part in range(2):
-        known = jnp.broadcast_to(trig_ref[part : part + 1, :], (8, LANES))
+        row = jnp.broadcast_to(known[part : part + 1, :], (8, LANES))
         for block in range(rows // 8):
             yaw_ref[part, block * 8 : block * 8 + 8, :] = lane_take(
-                known, who[block * 8 : block * 8 + 8]
+                row, who[block * 8 : block * 8 + 8]
             )
-    entries = load_entries(params_ref, scr, rows)
+    entries = [scr[pl.ds(row * rows, rows), :] for row in range(NPAR)]
     for quantity, value in enumerate(project(entries, yaw_ref[0], yaw_ref[1])):
         table[pl.ds(quantity * rows, rows), :] = value
 
+
+def look_up(rows, chunks, column_ref, place, eight_ref, one_ref, table):
     def table_eight(chunk):
         return table[pl.ds(chunk, 8, stride=rows), :]
 
     def table_one(block):
         return table[pl.ds(8 * rows + block * 8, 8), :]
+
+    index = jnp.broadcast_to(column_ref[:, place], (8, LANES))
+    eight_ref[:, place], one_ref[:, place] = gather_columns(
+        index, table_eight, table_one, chunks + 1
+    )
+
+
+def owner_kernel(
+    cap, rows, params_ref, column_ref, views_ref, trig_ref, eight_ref, one_ref, yaw_ref, scr, table
+):
+    slots = column_ref.shape[1]
+    chunks = params_ref.shape[1] // LANES
+    clear_entries(scr, rows)
+    load_entries(params_ref, scr, rows)
+    project_all(
+        cap, rows, params_ref, column_ref, views_ref[...], trig_ref[...], yaw_ref, scr, table
+    )
 
     @pl.loop(0, slots // LANES)
     def _(part):
         place = pl.ds(pl.multiple_of(part * LANES, LANES), LANES)
-        index = jnp.broadcast_to(column_ref[:, place], (8, LANES))
-        eight, one = gather_columns(index, table_eight, table_one, chunks + 1)
-        eight_ref[:, place] = eight
-        one_ref[:, place] = one
+        look_up(rows, chunks, column_ref, place, eight_ref, one_ref, table)
+
+
+def owner_exchange_kernel(
+    owners,
+    render,
+    cap,
+    rows,
+    params_ref,
+    request_ref,
+    trig_ref,
+    eight_ref,
+    one_ref,
+    yaw_ref,
+    column_ref,
+    scr,
+    table,
+    got,
+    eight_sent,
+    one_sent,
+    *sems,
+):
+    peers = Peers(owners, render)
+    peers.greet()
+    held = params_ref.shape[1]
+    chunks = held // LANES
+    width = request_ref.shape[1] // owners
+    clear_entries(scr, rows)
+    peers.met()
+    asked = [peers.copy(request_ref, got, sems[:2], step, 0) for step in range(1, owners)]
+    for copy in asked:
+        copy.start()
+    peers.keep(request_ref, got)
+    load_entries(params_ref, scr, rows)
+    for copy in asked:
+        copy.wait()
+    lane = lax.broadcasted_iota(jnp.int32, (1, LANES), 1)
+    views = jnp.zeros((1, LANES), jnp.int32)
+    for peer in range(owners):
+        index = got[:, peer * width : peer * width + cap]
+        column_ref[:, peer * cap : (peer + 1) * cap] = jnp.where(index == 0, held + peer, index)
+        views = jnp.where(lane == peer, got[:, peer * width + cap : (peer + 1) * width], views)
+    project_all(cap, rows, params_ref, column_ref, views, trig_ref[...], yaw_ref, scr, table)
+
+    def block(peer):
+        for part in range(cap // LANES):
+            place = pl.ds(pl.multiple_of(peer * cap + part * LANES, LANES), LANES)
+            look_up(rows, chunks, column_ref, place, eight_sent, one_sent, table)
+
+    def pairs(step):
+        return [
+            peers.copy(eight_sent, eight_ref, sems[2:], step, 0),
+            peers.copy(one_sent, one_ref, sems[2:], step, 1),
+        ]
+
+    @pl.loop(1, owners)
+    def _(step):
+        block(peers.peer(step))
+        for copy in pairs(step):
+            copy.start()
+
+    block(peers.me)
+    peers.keep(eight_sent, eight_ref)
+    peers.keep(one_sent, one_ref)
+    for step in range(1, owners):
+        for copy in pairs(step):
+            copy.wait()
 
 
 def tile_kernel(
+    owners,
+    render,
     eight_ref,
     one_ref,
     slots_ref,
@@ -257,6 +385,14 @@
     one_table,
     *banks,
 ):
+    fused = owners > 0
+    if fused:
+        *banks, eight_sent, one_sent, send_sem, recv_sem = banks
+        sems = (send_sem, recv_sem)
+        peers = Peers(owners, render)
+        peers.greet()
+    else:
+        eight_sent, one_sent = grad_eight_ref, grad_one_ref
     tiles, length = slots_ref.shape
     slots = eight_ref.shape[1]
     chunks = slots // LANES
@@ -399,15 +535,27 @@
                 next(one)
 
     for chunk in range(chunks):
-        grad_eight_ref[:, chunk * LANES : (chunk + 1) * LANES] = total[pl.ds(chunk, 8, stride=rows), :]
-        grad_one_ref[:, chunk * LANES : (chunk + 1) * LANES] = total[pl.ds(8 * rows + chunk, 1), :]
+        eight_sent[:, chunk * LANES : (chunk + 1) * LANES] = total[pl.ds(chunk, 8, stride=rows), :]
+        one_sent[:, chunk * LANES : (chunk + 1) * LANES] = total[pl.ds(8 * rows + chunk, 1), :]
+    if fused:
+        peers.met()
+        copies = []
+        for step in range(1, owners):
+            copies.append(peers.copy(eight_sent, grad_eight_ref, sems, step, 0))
+            copies.append(peers.copy(one_sent, grad_one_ref, sems, step, 1))
+        for copy in copies:
+            copy.start()
+        peers.keep(eight_sent, grad_eight_ref)
+        peers.keep(one_sent, grad_one_ref)
+        for copy in copies:
+            copy.wait()
 
 
 def update_kernel(
     rows,
     params_ref,
-    first_ref,
-    second_ref,
+    first_hbm,
+    second_hbm,
     column_ref,
     yaw_ref,
     eight_ref,
@@ -417,13 +565,21 @@
     new_second_ref,
     scr,
     total,
+    first_ref,
+    second_ref,
+    load_sem,
 ):
     slots = column_ref.shape[1]
     chunks = params_ref.shape[1] // LANES
-    for row in range(NPAR):
-        scr[pl.ds(row * rows, rows), :] = jnp.ones((rows, LANES), jnp.float32)
+    clear_entries(scr, rows)
     total[...] = jnp.zeros_like(total)
     width = 256
+    moments_in = [
+        pltpu.make_async_copy(first_hbm, first_ref, load_sem.at[0]),
+        pltpu.make_async_copy(second_hbm, second_ref, load_sem.at[1]),
+    ]
+    for copy in moments_in:
+        copy.start()
 
     @pl.loop(0, slots // width)
     def _(part):
@@ -451,6 +607,8 @@
     rates = jnp.where(row_index < 3, 0.00016, rates)
     fix_one = 1.0 - beta_one**ADAM_STEP
     fix_two = 1.0 - beta_two**ADAM_STEP
+    for copy in moments_in:
+        copy.wait()
     for chunk in range(chunks):
         place = slice(chunk * LANES, (chunk + 1) * LANES)
         gradient = scr[pl.ds(chunk, NPAR, stride=rows), :]
@@ -464,59 +622,7 @@
         new_second_ref[:, place] = variance
 
 
-def exchange_kernel(owners, render, *refs):
-    count = (len(refs) - 2) // 2
-    sources, landings, (send_sem, recv_sem) = refs[:count], refs[count : 2 * count], refs[2 * count :]
-    me = lax.axis_index("owner") * render + lax.axis_index("render")
-
-    def place(ref, peer):
-        width = ref.shape[1] // owners
-        return ref.at[:, pl.ds(pl.multiple_of(peer * width, LANES), width)]
-
-    def where(step):
-        peer = lax.rem(me + step, owners)
-        return peer, {"owner": lax.div(peer, render), "render": lax.rem(peer, render)}
-
-    barrier = pltpu.get_barrier_semaphore()
-    for step in range(1, owners):
-        pl.semaphore_signal(
-            barrier, inc=1, device_id=where(step)[1], device_id_type=pl.DeviceIdType.MESH
-        )
-    pl.semaphore_wait(barrier, owners - 1)
-    copies = []
-    for step in range(1, owners):
-        peer, device = where(step)
-        for item in range(count):
-            copy = pltpu.make_async_remote_copy(
-                src_ref=place(sources[item], peer),
-                dst_ref=place(landings[item], me),
-                send_sem=send_sem.at[step, item],
-                recv_sem=recv_sem.at[step, item],
-                device_id=device,
-                device_id_type=pl.DeviceIdType.MESH,
-            )
-            copy.start()
-            copies.append(copy)
-    for item in range(count):
-        width = sources[item].shape[1] // owners
-        own = pl.ds(pl.multiple_of(me * width, LANES), width)
-        landings[item][:, own] = sources[item][:, own]
-    for copy in copies:
-        copy.wait()
-
-
-def exchange(arrays, owners, render, number):
-    if arrays[0].shape[1] // owners % LANES == 0:
-        vmem = pl.BlockSpec(memory_space=pltpu.VMEM)
-        return pl.pallas_call(
-            functools.partial(exchange_kernel, owners, render),
-            out_shape=[jax.ShapeDtypeStruct(each.shape, each.dtype) for each in arrays],
-            in_specs=[vmem] * len(arrays),
-            out_specs=[vmem] * len(arrays),
-            scratch_shapes=[pltpu.SemaphoreType.DMA((owners, len(arrays)))] * 2,
-            compiler_params=pltpu.CompilerParams(collective_id=number, has_side_effects=True),
-            name=f"exchange_{number}",
-        )(*arrays)
+def exchange(arrays, owners):
     counts = [each.shape[0] for each in arrays]
     values = jnp.concatenate(arrays, axis=0)
     sent = values.reshape(values.shape[0], owners, -1)
@@ -538,34 +644,52 @@
     rows = (chunks + 1 + 7) // 8 * 8
     f32 = jnp.float32
     view = tile_ids[0] // tiles_view
-    spare = LANES if cap % LANES == 0 else 1
+    vmem = pl.BlockSpec(memory_space=pltpu.VMEM)
+    fused = cap % LANES == 0
+    trig = jnp.stack([jnp.cos(view_yaw), jnp.sin(view_yaw)])
+    trig = jnp.pad(trig, ((0, 6), (0, LANES - view_yaw.shape[0])))
+    spare = LANES if fused else 1
     requests = jnp.concatenate([visible[0], jnp.full((owners, spare), view, jnp.int32)], axis=1)
-    (wanted,) = exchange([requests.reshape(1, -1)], owners, render, 0)
-    wanted = wanted.reshape(owners, cap + spare)
-    index = wanted[:, :cap]
-    asker = jnp.arange(owners, dtype=jnp.int32)[:, None]
-    column = jnp.where(index == 0, held + asker, index).reshape(1, slots)
-    view_ids = jnp.arange(view_yaw.shape[0], dtype=jnp.int32)
-    yaw = jnp.sum(jnp.where(wanted[:, cap][:, None] == view_ids[None, :], view_yaw[None, :], 0.0), axis=1)
-    trig = jnp.stack([jnp.cos(yaw), jnp.sin(yaw)])
-    trig = jnp.pad(trig, ((0, 6), (0, LANES - owners)))
-    eight, one, yaws = pl.pallas_call(
-        functools.partial(owner_kernel, cap, rows),
-        out_shape=[
-            jax.ShapeDtypeStruct((8, slots), f32),
-            jax.ShapeDtypeStruct((1, slots), f32),
-            jax.ShapeDtypeStruct((2, rows, LANES), f32),
-        ],
-        scratch_shapes=[pltpu.VMEM((NPAR * rows, LANES), f32), pltpu.VMEM((QUANT * rows, LANES), f32)],
-        compiler_params=VMEM,
-        name="owner_project",
-    )(params, column, trig)
-    eight, one = exchange([eight, one], owners, render, 1)
+    requests = requests.reshape(1, -1)
+    shared = [
+        jax.ShapeDtypeStruct((8, slots), f32),
+        jax.ShapeDtypeStruct((1, slots), f32),
+        jax.ShapeDtypeStruct((2, rows, LANES), f32),
+    ]
+    room = [pltpu.VMEM((NPAR * rows, LANES), f32), pltpu.VMEM((QUANT * rows, LANES), f32)]
+    sends = [pltpu.VMEM((8, slots), f32), pltpu.VMEM((1, slots), f32)]
+    sems = [pltpu.SemaphoreType.DMA((owners, 2))] * 2
+    if fused:
+        eight, one, yaws, column = pl.pallas_call(
+            functools.partial(owner_exchange_kernel, owners, render, cap, rows),
+            out_shape=shared + [jax.ShapeDtypeStruct((1, slots), jnp.int32)],
+            in_specs=[vmem] * 3,
+            out_specs=[vmem] * 4,
+            scratch_shapes=room + [pltpu.VMEM(requests.shape, jnp.int32)] + sends + sems + sems,
+            compiler_params=pltpu.CompilerParams(
+                vmem_limit_bytes=56 * 1024 * 1024, collective_id=0, has_side_effects=True
+            ),
+            name="owner_project",
+        )(params, requests, trig)
+    else:
+        (wanted,) = exchange([requests], owners)
+        wanted = wanted.reshape(owners, cap + spare)
+        index = wanted[:, :cap]
+        asker = jnp.arange(owners, dtype=jnp.int32)[:, None]
+        column = jnp.where(index == 0, held + asker, index).reshape(1, slots)
+        views = jnp.pad(wanted[:, cap], (0, LANES - owners)).reshape(1, LANES)
+        eight, one, yaws = pl.pallas_call(
+            functools.partial(owner_kernel, cap, rows),
+            out_shape=shared,
+            scratch_shapes=room,
+            compiler_params=VMEM,
+            name="owner_project",
+        )(params, column, views, trig)
+        eight, one = exchange([eight, one], owners)
     within = tile_ids % tiles_view
     anchors = jnp.stack([within % tiles_across, within // tiles_across]).astype(f32) * 16.0 + 8.0
-    vmem = pl.BlockSpec(memory_space=pltpu.VMEM)
     rendered, grad_eight, grad_one = pl.pallas_call(
-        tile_kernel,
+        functools.partial(tile_kernel, owners if fused else 0, render),
         out_shape=[
             jax.ShapeDtypeStruct(target.shape, f32),
             jax.ShapeDtypeStruct((8, slots), f32),
@@ -582,15 +706,28 @@
             pltpu.VMEM((2 * PIX, length), jnp.bfloat16),
             pltpu.VMEM((2 * PIX, length), jnp.bfloat16),
         ]
-        * (2 if tiles % 2 == 0 else 1),
-        compiler_params=VMEM,
+        * (2 if tiles % 2 == 0 else 1)
+        + (sends + sems if fused else []),
+        compiler_params=pltpu.CompilerParams(
+            vmem_limit_bytes=56 * 1024 * 1024, collective_id=1, has_side_effects=True
+        )
+        if fused
+        else VMEM,
         name="tile_step",
     )(eight, one, tile_slots, depth_rank, anchors, target)
-    grad_eight, grad_one = exchange([grad_eight, grad_one], owners, render, 2)
+    if not fused:
+        grad_eight, grad_one = exchange([grad_eight, grad_one], owners)
+    hbm = pl.BlockSpec(memory_space=pl.ANY)
     new_params, new_first, new_second = pl.pallas_call(
         functools.partial(update_kernel, rows),
         out_shape=[jax.ShapeDtypeStruct(params.shape, f32)] * 3,
-        scratch_shapes=[pltpu.VMEM((NPAR * rows, LANES), f32), pltpu.VMEM((QUANT * rows, LANES), f32)],
+        in_specs=[vmem, hbm, hbm, vmem, vmem, vmem, vmem],
+        scratch_shapes=room
+        + [
+            pltpu.VMEM(params.shape, f32),
+            pltpu.VMEM(params.shape, f32),
+            pltpu.SemaphoreType.DMA((2,)),
+        ],
         compiler_params=VMEM,
         name="adam_step",
     )(params, first_moment, second_moment, column, yaws, grad_eight, grad_one)

time: 73.4 us -> 58.6 us (0.80)
  Pallas kernels: 66 us -> 53.8 us
  other arithmetic: 2.91 us -> 1.21 us
    pallas_call x5 -> x2, Pallas kernels: 56.3 us -> 44.8 us  [the longest x1 25.7 us: body(): pl.pallas_call(functools.partial(tile_kernel, owners if fused else 0, ren...]
    pallas_call x1 -> x0, other arithmetic: 1.44 us -> none  [exchange(): pl.pallas_call(functools.partial(exchange_kernel, owners, render), out_sh...]
    pallas_call x1, Pallas kernels: 9.7 us -> 8.97 us  [body(): pl.pallas_call(functools.partial(update_kernel, rows), out_shape=[jax.Sha...]
    unnamed x10 -> x11, local copies, waits for them, and re-layouts: 2.64 us -> 2.51 us
where the time goes in v3:
time: 58.6 us; the launch traced here: 58.4 us
  Pallas kernels  53.8 us (92%)
  local copies, waits for them, and re-layouts  2.55 us (4%)
  other arithmetic  1.21 us (2%)
  between operations  0.83 us (1%)
    pallas_call x1, Pallas kernels, body(): pl.pallas_call(functools.partial(tile_kernel, owners if fused else 0, ren...  25.7 us
    pallas_call x1, Pallas kernels, body(): pl.pallas_call(functools.partial(owner_exchange_kernel, owners, render, c...  19.1 us
    pallas_call x1, Pallas kernels, body(): pl.pallas_call(functools.partial(update_kernel, rows), out_shape=[jax.Sha...  8.97 us
    unnamed x11, local copies, waits for them, and re-layouts  2.51 us

profile of v3, /device:TPU:0, one launch (start us, length us, event | category | flops | bytes accessed | tf_op | source)
XLA Modules:
  0.0 58.4 jit_solution(4542118473941359690)
XLA Ops:
  0.6 0.0 copy-start.3
  0.6 0.6 %copy-done.3 = s32[16]{0:T(128)S(1)} copy-done((s32[16]{0:T(128)S(1)}, s32[16]{0:T(128)}, u32[]{:S(2)}) %copy-start.3) | copy-done | bytes 88
  1.4 0.0 copy-start.2
  1.4 0.0 copy-start.1
  1.4 0.6 %copy-done.2 = f32[16]{0:T(128)S(1)} copy-done((f32[16]{0:T(128)S(1)}, f32[16]{0:T(128)}, u32[]{:S(2)}) %copy-start.2) | copy-done | bytes 88
  2.1 0.6 fusion.1.anchor_ref
  2.7 0.6 %select_maximum_fusion.trig_ref = f32[8,128]{1,0:T(8,128)} fusion(f32[1,16]{1,0:T(1,128)S(1)} %get-tuple-element.27, f32[1,16]{1,0:T(1,128)S(1)} %get-tuple-element.26), kind=kLoop, calls=%fused_computation.1 | loop fusion | flops 8192 | bytes 4224 | tf_op jit(solution)/shard_map/stack | solution.py:649
  3.3 0.0 copy-done.1
  3.3 0.6 %copy.13 = s32[1,1,16,384]{3,1,2,0:T(1,128)} copy(s32[1,1,16,384]{3,2,1,0:T(8,128)S(1)} %pad_bitcast_fusion) | data formatting | bytes 49152
  3.9 19.1 %owner_project.1 = (f32[8,4096]{1,0:T(8,128)}, f32[1,4096]{1,0:T(1,128)}, f32[2,40,128]{2,1,0:T(8,128)}, s32[1,4096]{1,0:T(1,128)}) custom-call(f32[59,4096]{1,0:T(8,128)} %params_ref.3, s32[1,6144]{1,0:T(1,128)} %bitcast.16, f32[8,128]{1,0:T(8,128)} %select_maximum_fusion.trig_ref), custom_call_target="tpu_custom_call" | custom-call | tf_op jit(solution)/shard_map/owner_project/pallas_call | solution.py:663
  23.0 25.7 %tile_step.1 = (f32[3,16,256]{2,1,0:T(8,128)}, f32[8,4096]{1,0:T(8,128)}, f32[1,4096]{1,0:T(1,128)}) custom-call(f32[8,4096]{1,0:T(8,128)} %get-tuple-element.16.eight_ref, f32[1,4096]{1,0:T(1,128)} %get-tuple-element.17.one_ref, s32[16,256]{1,0:T(8,128)} %slots_ref.1, s32[16,256]{1,0:T(8,128)} %rank_ref.1, f32[2,16]{1,0:T(2,128)} %fusion.1.anchor_ref, ...), custom_call_target="tpu_custom_call" | custom-call | tf_op jit(solution)/shard_map/tile_step/pallas_call | solution.py:691
  48.8 0.0 copy-start
  48.8 9.0 %adam_step.1 = (f32[59,4096]{1,0:T(8,128)}, f32[59,4096]{1,0:T(8,128)}, f32[59,4096]{1,0:T(8,128)}) custom-call(f32[59,4096]{1,0:T(8,128)} %params_ref.3, f32[59,4096]{1,0:T(8,128)} %first_hbm.1, f32[59,4096]{1,0:T(8,128)} %second_hbm.1, s32[1,4096]{1,0:T(1,128)} %get-tuple-element.14.column_ref, f32[2,40,128]{2,1,0:T(8,128)} %get-tuple-element.15.yaw_ref, ...), custom_call_target="tpu_custom_call" | custom-call | tf_op jit(solution)/shard_map/adam_step/pallas_call | solution.py:721
  57.7 0.0 copy-done
  57.7 0.6 %copy.15 = f32[3,16,256]{2,1,0:T(8,128)} copy(f32[3,16,256]{2,1,0:T(8,128)S(1)} %copy-done) | data formatting | bytes 98304
  (4 shorter events, 0.1 us)
Async XLA Ops:
  0.6 0.7 %copy-start.3 = (s32[16]{0:T(128)S(1)}, s32[16]{0:T(128)}, u32[]{:S(2)}) copy-start(s32[16]{0:T(128)} %param.14) | copy-start | bytes 196
  1.4 0.7 %copy-start.2 = (f32[16]{0:T(128)S(1)}, f32[16]{0:T(128)}, u32[]{:S(2)}) copy-start(f32[16]{0:T(128)} %param.13) | copy-start | bytes 196
  1.4 1.9 %copy-start.1 = (s32[1,16,256]{2,1,0:T(8,128)S(1)}, s32[1,16,256]{2,1,0:T(8,128)}, u32[]{:S(2)}) copy-start(s32[1,16,256]{2,1,0:T(8,128)} %param.15) | copy-start | bytes 49156
  48.8 9.0 %copy-start = (f32[3,16,256]{2,1,0:T(8,128)S(1)}, f32[3,16,256]{2,1,0:T(8,128)}, u32[]{:S(2)}) copy-start(f32[3,16,256]{2,1,0:T(8,128)} %get-tuple-element.35) | copy-start | bytes 147460

commit v4 on v3

--- a/solution.py
+++ b/solution.py
@@ -309,14 +309,16 @@
     cap,
     rows,
     params_ref,
-    request_ref,
-    trig_ref,
+    visible_ref,
+    yaw_in_ref,
+    tile_ref,
     eight_ref,
     one_ref,
     yaw_ref,
     column_ref,
     scr,
     table,
+    request_ref,
     got,
     eight_sent,
     one_sent,
@@ -327,6 +329,10 @@
     held = params_ref.shape[1]
     chunks = held // LANES
     width = request_ref.shape[1] // owners
+    view = jnp.full((1, LANES), tile_ref[0] // tiles_view, jnp.int32)
+    for peer in range(owners):
+        request_ref[:, peer * width : peer * width + cap] = visible_ref[0, peer : peer + 1, :]
+        request_ref[:, peer * width + cap : (peer + 1) * width] = view
     clear_entries(scr, rows)
     peers.met()
     asked = [peers.copy(request_ref, got, sems[:2], step, 0) for step in range(1, owners)]
@@ -334,6 +340,12 @@
         copy.start()
     peers.keep(request_ref, got)
     load_entries(params_ref, scr, rows)
+    side = lax.broadcasted_iota(jnp.int32, (8, LANES), 0)
+    wide = lax.broadcasted_iota(jnp.int32, (8, LANES), 1)
+    yaw = jnp.zeros((8, LANES), jnp.float32)
+    for each in range(yaw_in_ref.shape[0]):
+        yaw = jnp.where(wide == each, yaw_in_ref[each], yaw)
+    trig = jnp.where(side == 0, jnp.cos(yaw), jnp.sin(yaw))
     for copy in asked:
         copy.wait()
     lane = lax.broadcasted_iota(jnp.int32, (1, LANES), 1)
@@ -342,7 +354,7 @@
         index = got[:, peer * width : peer * width + cap]
         column_ref[:, peer * cap : (peer + 1) * cap] = jnp.where(index == 0, held + peer, index)
         views = jnp.where(lane == peer, got[:, peer * width + cap : (peer + 1) * width], views)
-    project_all(cap, rows, params_ref, column_ref, views, trig_ref[...], yaw_ref, scr, table)
+    project_all(cap, rows, params_ref, column_ref, views, trig, yaw_ref, scr, table)
 
     def block(peer):
         for part in range(cap // LANES):
@@ -376,7 +388,7 @@
     one_ref,
     slots_ref,
     rank_ref,
-    anchor_ref,
+    tile_ref,
     target_ref,
     out_ref,
     grad_eight_ref,
@@ -447,8 +459,11 @@
         ordered = jnp.concatenate(ordered, axis=1)
         eight = jnp.concatenate(eights, axis=1)
         one = jnp.concatenate(ones, axis=1)
-        off_u = eight[0:1] - anchor_ref[0, tile]
-        off_v = eight[1:2] - anchor_ref[1, tile]
+        within = lax.rem(tile_ref[tile], tiles_view)
+        corner_x = lax.rem(within, tiles_across) * 16
+        corner_y = lax.div(within, tiles_across) * 16
+        off_u = eight[0:1] - (corner_x.astype(jnp.float32) + 8.0)
+        off_v = eight[1:2] - (corner_y.astype(jnp.float32) + 8.0)
         con_a, con_b, con_c = eight[2:3], eight[3:4], eight[4:5]
         lin_x = con_a * off_u + con_b * off_v
         lin_y = con_b * off_u + con_c * off_v
@@ -573,7 +588,7 @@
     chunks = params_ref.shape[1] // LANES
     clear_entries(scr, rows)
     total[...] = jnp.zeros_like(total)
-    width = 256
+    width = 1024
     moments_in = [
         pltpu.make_async_copy(first_hbm, first_ref, load_sem.at[0]),
         pltpu.make_async_copy(second_hbm, second_ref, load_sem.at[1]),
@@ -643,14 +658,9 @@
     chunks = held // LANES
     rows = (chunks + 1 + 7) // 8 * 8
     f32 = jnp.float32
-    view = tile_ids[0] // tiles_view
     vmem = pl.BlockSpec(memory_space=pltpu.VMEM)
     fused = cap % LANES == 0
-    trig = jnp.stack([jnp.cos(view_yaw), jnp.sin(view_yaw)])
-    trig = jnp.pad(trig, ((0, 6), (0, LANES - view_yaw.shape[0])))
-    spare = LANES if fused else 1
-    requests = jnp.concatenate([visible[0], jnp.full((owners, spare), view, jnp.int32)], axis=1)
-    requests = requests.reshape(1, -1)
+    smem = pl.BlockSpec(memory_space=pltpu.SMEM)
     shared = [
         jax.ShapeDtypeStruct((8, slots), f32),
         jax.ShapeDtypeStruct((1, slots), f32),
@@ -663,17 +673,25 @@
         eight, one, yaws, column = pl.pallas_call(
             functools.partial(owner_exchange_kernel, owners, render, cap, rows),
             out_shape=shared + [jax.ShapeDtypeStruct((1, slots), jnp.int32)],
-            in_specs=[vmem] * 3,
+            in_specs=[vmem, vmem, smem, smem],
             out_specs=[vmem] * 4,
-            scratch_shapes=room + [pltpu.VMEM(requests.shape, jnp.int32)] + sends + sems + sems,
+            scratch_shapes=room
+            + [pltpu.VMEM((1, owners * (cap + LANES)), jnp.int32)] * 2
+            + sends
+            + sems
+            + sems,
             compiler_params=pltpu.CompilerParams(
                 vmem_limit_bytes=56 * 1024 * 1024, collective_id=0, has_side_effects=True
             ),
             name="owner_project",
-        )(params, requests, trig)
+        )(params, visible, view_yaw, tile_ids)
     else:
+        trig = jnp.stack([jnp.cos(view_yaw), jnp.sin(view_yaw)])
+        trig = jnp.pad(trig, ((0, 6), (0, LANES - view_yaw.shape[0])))
+        view = jnp.full((owners, 1), tile_ids[0] // tiles_view, jnp.int32)
+        requests = jnp.concatenate([visible[0], view], axis=1).reshape(1, -1)
         (wanted,) = exchange([requests], owners)
-        wanted = wanted.reshape(owners, cap + spare)
+        wanted = wanted.reshape(owners, cap + 1)
         index = wanted[:, :cap]
         asker = jnp.arange(owners, dtype=jnp.int32)[:, None]
         column = jnp.where(index == 0, held + asker, index).reshape(1, slots)
@@ -686,8 +704,6 @@
             name="owner_project",
         )(params, column, views, trig)
         eight, one = exchange([eight, one], owners)
-    within = tile_ids % tiles_view
-    anchors = jnp.stack([within % tiles_across, within // tiles_across]).astype(f32) * 16.0 + 8.0
     rendered, grad_eight, grad_one = pl.pallas_call(
         functools.partial(tile_kernel, owners if fused else 0, render),
         out_shape=[
@@ -695,7 +711,7 @@
             jax.ShapeDtypeStruct((8, slots), f32),
             jax.ShapeDtypeStruct((1, slots), f32),
         ],
-        in_specs=[vmem, vmem, vmem, vmem, pl.BlockSpec(memory_space=pltpu.SMEM), vmem],
+        in_specs=[vmem, vmem, vmem, vmem, smem, vmem],
         scratch_shapes=[
             pltpu.VMEM((QUANT * slots // LANES, LANES), f32),
             pltpu.VMEM((slots // LANES, LANES), f32),
@@ -706,7 +722,7 @@
             pltpu.VMEM((2 * PIX, length), jnp.bfloat16),
             pltpu.VMEM((2 * PIX, length), jnp.bfloat16),
         ]
-        * (2 if tiles % 2 == 0 else 1)
+        * (8 if tiles % 8 == 0 else 1)
         + (sends + sems if fused else []),
         compiler_params=pltpu.CompilerParams(
             vmem_limit_bytes=56 * 1024 * 1024, collective_id=1, has_side_effects=True
@@ -714,7 +730,7 @@
         if fused
         else VMEM,
         name="tile_step",
-    )(eight, one, tile_slots, depth_rank, anchors, target)
+    )(eight, one, tile_slots, depth_rank, tile_ids, target)
     if not fused:
         grad_eight, grad_one = exchange([grad_eight, grad_one], owners)
     hbm = pl.BlockSpec(memory_space=pl.ANY)

time: 58.6 us -> 46.9 us (0.80)
  Pallas kernels: 53.8 us -> 45.4 us
  local copies, waits for them, and re-layouts: 2.55 us -> 0.63 us
  other arithmetic: 1.21 us -> 0 us
    pallas_call x1, Pallas kernels: 25.7 us -> 19.3 us  [body(): pl.pallas_call(functools.partial(tile_kernel, owners if fused else 0, ren...]
    pallas_call x1, Pallas kernels: 8.97 us -> 6.92 us  [body(): pl.pallas_call(functools.partial(update_kernel, rows), out_shape=[jax.Sha...]
    unnamed x11 -> x3, local copies, waits for them, and re-layouts: 2.51 us -> 0.63 us
    another operation x3 -> x0, other arithmetic: 0.63 us -> none  [the longest x1 0.6 us: body(): trig = jnp.stack([jnp.cos(view_yaw), jnp.sin(view_yaw)])]
where the time goes in v4:
time: 46.9 us; the launch traced here: 46.7 us
  Pallas kernels  45.4 us (97%)
  between operations  0.67 us (1%)
  local copies, waits for them, and re-layouts  0.63 us (1%)
    pallas_call x1, Pallas kernels, body(): pl.pallas_call(functools.partial(tile_kernel, owners if fused else 0, ren...  19.3 us
    pallas_call x1, Pallas kernels, body(): pl.pallas_call(functools.partial(owner_exchange_kernel, owners, render, c...  19.1 us
    pallas_call x1, Pallas kernels, body(): pl.pallas_call(functools.partial(update_kernel, rows), out_shape=[jax.Sha...  6.92 us

profile of v4, /device:TPU:0, one launch (start us, length us, event | category | flops | bytes accessed | tf_op | source)
XLA Modules:
  0.0 46.7 jit_solution(5603282933005105124)
XLA Ops:
  0.6 19.1 %owner_project.1 = (f32[8,4096]{1,0:T(8,128)}, f32[1,4096]{1,0:T(1,128)}, f32[2,40,128]{2,1,0:T(8,128)}, s32[1,4096]{1,0:T(1,128)}) custom-call(f32[59,4096]{1,0:T(8,128)} %params_ref.3, s32[1,16,256]{2,1,0:T(8,128)} %visible_ref.1, f32[16]{0:T(128)} %yaw_in_ref.1, s32[16]{0:T(128)} %tile_ref.3), custom_call_target="tpu_custom_call" | custom-call | tf_op jit(solution)/shard_map/owner_project/pallas_call | solution.py:673
  19.8 19.3 %tile_step.1 = (f32[3,16,256]{2,1,0:T(8,128)}, f32[8,4096]{1,0:T(8,128)}, f32[1,4096]{1,0:T(1,128)}) custom-call(f32[8,4096]{1,0:T(8,128)} %get-tuple-element.16.eight_ref, f32[1,4096]{1,0:T(1,128)} %get-tuple-element.17.one_ref, s32[16,256]{1,0:T(8,128)} %slots_ref.1, s32[16,256]{1,0:T(8,128)} %rank_ref.1, s32[16]{0:T(128)} %tile_ref.3, ...), custom_call_target="tpu_custom_call" | custom-call | tf_op jit(solution)/shard_map/tile_step/pallas_call | solution.py:707
  39.1 0.0 copy-start
  39.1 6.9 %adam_step.1 = (f32[59,4096]{1,0:T(8,128)}, f32[59,4096]{1,0:T(8,128)}, f32[59,4096]{1,0:T(8,128)}) custom-call(f32[59,4096]{1,0:T(8,128)} %params_ref.3, f32[59,4096]{1,0:T(8,128)} %first_hbm.1, f32[59,4096]{1,0:T(8,128)} %second_hbm.1, s32[1,4096]{1,0:T(1,128)} %get-tuple-element.14.column_ref, f32[2,40,128]{2,1,0:T(8,128)} %get-tuple-element.15.yaw_ref, ...), custom_call_target="tpu_custom_call" | custom-call | tf_op jit(solution)/shard_map/adam_step/pallas_call | solution.py:737
  46.0 0.0 copy-done
  46.1 0.6 %copy.14 = f32[3,16,256]{2,1,0:T(8,128)} copy(f32[3,16,256]{2,1,0:T(8,128)S(1)} %copy-done) | data formatting | bytes 98304
Async XLA Ops:
  39.1 6.9 %copy-start = (f32[3,16,256]{2,1,0:T(8,128)S(1)}, f32[3,16,256]{2,1,0:T(8,128)}, u32[]{:S(2)}) copy-start(f32[3,16,256]{2,1,0:T(8,128)} %get-tuple-element.31) | copy-start | bytes 147460
